TPU v7x, 128 devices: a whole 4x4x4 slice. The times are simulated.
128 devices in a mesh: seq: 32 (over z, x, core), batch: 4 (over y).
Axes of the slice: x: 4, y: 4, z: 4, core: 2. Of those that a mesh axis runs over, the one named last changes fastest.
Arguments:
- inputs: bfloat16 [131072, 768], P(('batch', 'seq')), parts along dimension 0, may hold values from -6 to 6
- token_rates: float32 [131072], P(('batch', 'seq')), parts along dimension 0, may hold values from 0.1 to 1
- proj_query: bfloat16 [768, 256], replicated, may hold values from -0.21875 to 0.21875
- proj_key: bfloat16 [768, 256], replicated, may hold values from -0.21875 to 0.21875
- proj_value: bfloat16 [768, 256], replicated, may hold values from -0.21875 to 0.21875
- proj_output: bfloat16 [256, 768], replicated, may hold values from -0.375 to 0.375
- fast_in: float32 [256, 512], replicated, may hold values from -0.375 to 0.375
- fast_up: float32 [256, 512], replicated, may hold values from -0.375 to 0.375
- fast_out: float32 [512, 256], replicated, may hold values from -0.25 to 0.25
- cotangent: bfloat16 [131072, 768], P(('batch', 'seq')), parts along dimension 0, may hold values from -6 to 6
Outputs:
- back_inputs: bfloat16 [131072, 768], P(('batch', 'seq')), parts along dimension 0
- back_rate: float32 [131072], P(('batch', 'seq')), parts along dimension 0
- grad_in: float32 [1024, 512], P('batch'), parts along dimension 0
- grad_up: float32 [1024, 512], P('batch'), parts along dimension 0
- grad_out: float32 [2048, 256], P('batch'), parts along dimension 0
- grad_query: float32 [768, 1024], P('seq', 'batch'), parts along dimension 1
- grad_key: float32 [768, 1024], P('seq', 'batch'), parts along dimension 1
- grad_value: float32 [768, 1024], P('seq', 'batch'), parts along dimension 1
- grad_output: float32 [1024, 768], P('batch', 'seq'), parts along dimension 0
There are 4 independent parts, one for each index of `batch`. A program takes and returns all parts, laid end to end along the dimension named above; an argument that names none is the same for every part. Nothing has to cross between parts.
All inputs are finite; a program needn't handle non-finite values.
Results may differ from a plain program's by a relative error of at most 0.029.
Values may be sent and summed in bfloat16 or wider, within the bound.
No kernel may reach another device: no remote copies, remote signals or barrier semaphores. Data moves between devices by JAX's collectives and lax.ppermute only.
A program may use at most 128 MiB of HBM per device.

v0:
```python
import jax
import jax.numpy as jnp
from jax import lax
from jax.experimental import pallas as pl
from jax.experimental.pallas import tpu as pltpu
from jax.sharding import PartitionSpec as P

NS_STEPS = 5
TILE = 512
LARGE = 1024
F32 = jnp.float32
BF16 = jnp.bfloat16
VMEM_BYTES = 28 * 1024 * 1024


def rounded(value):
    return value.astype(jnp.bfloat16)


def product(left, right):
    return jnp.dot(left, right, preferred_element_type=jnp.float32)


def token_sum(left, right):
    return lax.dot_general(
        left, right, (((0,), (0,)), ((), ())), preferred_element_type=jnp.float32
    )


def times_transpose(left, right):
    return lax.dot_general(
        left, right, (((1,), (1,)), ((), ())), preferred_element_type=jnp.float32
    )


def sigmoid(value):
    return 1.0 / (1.0 + jnp.exp(-value))


def column(row):
    wide = jnp.broadcast_to(row, (128, row.shape[1])).T
    return jnp.concatenate([wide, wide], axis=1)


def rows_of(columns, tile=TILE):
    return pl.BlockSpec((tile, columns), lambda step: (step, 0))


def row_block(tile):
    return pl.BlockSpec((1, tile), lambda step: (0, step))


def whole(*shape):
    return pl.BlockSpec(shape, lambda step: (0,) * len(shape))


SCALAR = pl.BlockSpec(memory_space=pltpu.SMEM)
IN_VMEM = pl.BlockSpec(memory_space=pltpu.VMEM)


def params(limit=VMEM_BYTES):
    return pltpu.CompilerParams(vmem_limit_bytes=limit)


def cost(flops, moved):
    return pl.CostEstimate(flops=flops, bytes_accessed=moved, transcendentals=0)


def shape(dims, kind):
    return jax.ShapeDtypeStruct(dims, kind)


def add_sums(sums, parts):
    for index, part in enumerate(parts):
        rows = pl.ds(256 * index, 256)
        sums[rows, :] = sums[rows, :] + part


def put_sums(sums, parts):
    for index, part in enumerate(parts):
        sums[256 * index : 256 * index + 256, :] = part


def hand_halves(core_ref, sums, kept_ref, sent_ref):
    core = core_ref[0]
    kept_ref[...] = sums[pl.ds(pl.multiple_of(core * 384, 384), 384), :]
    sent_ref[...] = rounded(sums[pl.ds(pl.multiple_of((1 - core) * 384, 384), 384), :])


def first_step(action):
    pl.when(pl.program_id(0) == 0)(action)


def last_step(action):
    pl.when(pl.program_id(0) == pl.num_programs(0) - 1)(action)


def in_order(core_ref, own_ref, other_ref, pair):
    core = core_ref[0]
    pair[pl.ds(pl.multiple_of(core * 256, 256), 256), :] = own_ref[...]
    pair[pl.ds(pl.multiple_of((1 - core) * 256, 256), 256), :] = other_ref[...]


def share_rows(core, total, kept_ref, sent_ref, start):
    for a in range(4):
        for b in (0, 2):
            low = [pl.multiple_of(jnp.where(core == 0, (c * 4 + a) * 48, (a * 4 + c) * 48 + 24), 8) for c in (b, b + 1)]
            high = [pl.multiple_of(jnp.where(core == 0, (a * 4 + c) * 48 + 24, (c * 4 + a) * 48), 8) for c in (b, b + 1)]
            at = start + 24 * b
            kept_ref[a, at : at + 48, :] = jnp.concatenate([total[pl.ds(row, 24), :] for row in low], axis=0)
            sent_ref[a, at : at + 48, :] = rounded(jnp.concatenate([total[pl.ds(row, 24), :] for row in high], axis=0))


def update_kernel(core_ref, x_ref, rate_ref, pq_ref, pk_ref, pv_ref, fi_ref, fu_ref, fo_ref, q_ref, k_ref, v_ref, s_ref, kept_ref, sent_ref, sums, wi_ref, wu_ref, wo_ref):
    @first_step
    def _():
        sums[...] = jnp.zeros_like(sums)
        wi_ref[...] = rounded(fi_ref[...])
        wu_ref[...] = rounded(fu_ref[...])
        wo_ref[...] = rounded(fo_ref[...])

    x = x_ref[...]
    key_rows = rounded(product(x, pk_ref[...]))
    value_rows = rounded(product(x, pv_ref[...]))
    scaled = rounded(column(rate_ref[...]) * value_rows.astype(F32))
    q_ref[...] = rounded(product(x, pq_ref[...]))
    k_ref[...] = key_rows
    v_ref[...] = value_rows
    s_ref[...] = scaled
    pre_in = product(key_rows, wi_ref[...])
    pre_up = product(key_rows, wu_ref[...])
    upstream = times_transpose(scaled, wo_ref[...])
    sigma = sigmoid(pre_in)
    activation = pre_in * sigma
    slope = sigma * (1.0 + pre_in * (1.0 - sigma))
    hidden = rounded(activation * pre_up)
    grad_in_rows = rounded(upstream * pre_up * slope)
    grad_up_rows = rounded(upstream * activation)
    both = token_sum(key_rows, jnp.concatenate([grad_in_rows, grad_up_rows], axis=1))
    add_sums(sums, (both[:, :512], both[:, 512:], token_sum(scaled, hidden)))
    last_step(lambda: hand_halves(core_ref, sums, kept_ref, sent_ref))


WEIGHTS = [((256, 512), BF16), ((256, 512), BF16), ((512, 256), BF16)]


def update_rows(core, inputs, rates, proj_query, proj_key, proj_value, fast_in, fast_up, fast_out):
    tokens = inputs.shape[0]
    return pl.pallas_call(
        update_kernel,
        grid=(tokens // LARGE,),
        in_specs=[SCALAR, rows_of(768, LARGE), row_block(LARGE)] + [whole(768, 256)] * 3 + [ whole(256, 512), whole(256, 512), whole(512, 256)],
        out_specs=[rows_of(256, LARGE)] * 4 + [whole(384, 512)] * 2,
        out_shape=[shape((tokens, 256), BF16)] * 4 + [shape((384, 512), F32), shape((384, 512), BF16)],
        scratch_shapes=[pltpu.VMEM((768, 512), F32)] + [pltpu.VMEM(*w) for w in WEIGHTS],
        compiler_params=params(60 * 1024 * 1024),
        cost_estimate=cost(2400000000, 6000000),
        name="update_rows",
    )(core, inputs, rates, proj_query, proj_key, proj_value, fast_in, fast_up, fast_out)


def back_output_kernel(core_ref, c_ref, po_ref, fi_ref, fo_ref, out_ref, own_ref):
    core = core_ref[0]

    @first_step
    def _():
        own_ref[...] = jnp.where(core == 0, fi_ref[...], fo_ref[...].T)

    out_ref[...] = rounded(times_transpose(c_ref[...], po_ref[...]))


def back_output_rows(core, cotangent, proj_output, fast_in, fast_out):
    tokens = cotangent.shape[0]
    return pl.pallas_call(
        back_output_kernel,
        grid=(tokens // TILE,),
        in_specs=[SCALAR, rows_of(768), whole(256, 768), whole(256, 512), whole(512, 256)],
        out_specs=[rows_of(256), whole(256, 512)],
        out_shape=[shape((tokens, 256), BF16), shape((256, 512), F32)],
        compiler_params=params(),
        cost_estimate=cost(400000000, 4000000),
        name="back_output",
    )(core, cotangent, proj_output, fast_in, fast_out)


def query_kernel(core_ref, q_ref, bo_ref, own_ref, other_ref, nu_ref, bp_ref, br_ref, h_ref, kept_ref, sent_ref, sums, pair):
    in_order(core_ref, own_ref, other_ref, pair)
    query_rows, back_output = q_ref[...], bo_ref[...]
    pre_p = product(query_rows, pair[:256, :])
    pre_r = product(query_rows, nu_ref[...])
    back_hidden = product(back_output, pair[256:, :])
    sigma = sigmoid(pre_p)
    activation = pre_p * sigma
    slope = sigma * (1.0 + pre_p * (1.0 - sigma))
    hidden = rounded(activation * pre_r)
    back_p = rounded(back_hidden * pre_r * slope)
    back_r = rounded(back_hidden * activation)
    bp_ref[...] = back_p
    br_ref[...] = back_r
    h_ref[...] = hidden
    both = token_sum(query_rows, jnp.concatenate([back_p, back_r], axis=1))
    put_sums(sums, (both[:, :512], both[:, 512:], token_sum(back_output, hidden)))
    hand_halves(core_ref, sums, kept_ref, sent_ref)


def query_rows_back(core, query_rows, back_output, n_own, n_other, n_up):
    tokens = query_rows.shape[0]
    return pl.pallas_call(
        query_kernel,
        in_specs=[SCALAR] + [IN_VMEM] * 5,
        out_specs=[IN_VMEM] * 5,
        out_shape=[shape((tokens, 512), BF16)] * 3 + [shape((384, 512), F32), shape((384, 512), BF16)],
        scratch_shapes=[pltpu.VMEM((768, 512), F32), pltpu.VMEM((512, 512), BF16)],
        compiler_params=params(),
        cost_estimate=cost(1600000000, 6000000),
        name="query_rows_back",
    )(core, query_rows, back_output, n_own, n_other, n_up)


def out_grad_kernel(core_ref, h_ref, own_ref, other_ref, c_ref, kept_ref, sent_ref, go, pair):
    @first_step
    def _():
        in_order(core_ref, own_ref, other_ref, pair)
        go[...] = jnp.zeros_like(go)

    output_rows = rounded(times_transpose(h_ref[...], pair[256:, :]))
    go[...] += token_sum(c_ref[...], output_rows)

    @last_step
    def _():
        share_rows(core_ref[0], go, kept_ref, sent_ref, 0)


SHARES = [shape((4, 96, 256), F32), shape((4, 96, 256), BF16)]


def out_grads(core, hidden, n_own, n_other, cotangent):
    tokens = cotangent.shape[0]
    return pl.pallas_call(
        out_grad_kernel,
        grid=(tokens // TILE,),
        in_specs=[SCALAR, rows_of(512), whole(256, 512), whole(256, 512), rows_of(768)],
        out_specs=[whole(4, 96, 256)] * 2,
        out_shape=SHARES,
        scratch_shapes=[pltpu.VMEM((768, 256), F32), pltpu.VMEM((512, 512), BF16)],
        compiler_params=params(),
        cost_estimate=cost(700000000, 4000000),
        name="out_grads",
    )(core, hidden, n_own, n_other, cotangent)


def query_grad_kernel(core_ref, bp_ref, br_ref, own_ref, other_ref, nu_ref, x_ref, qg_ref, kept_ref, sent_ref, gq, pair):
    @first_step
    def _():
        in_order(core_ref, own_ref, other_ref, pair)
        gq[...] = jnp.zeros_like(gq)

    query_grad = rounded(times_transpose(bp_ref[...], pair[:256, :]) + times_transpose(br_ref[...], nu_ref[...]))
    qg_ref[...] = query_grad
    gq[...] += token_sum(x_ref[...], query_grad)

    @last_step
    def _():
        share_rows(core_ref[0], gq, kept_ref, sent_ref, 0)


def query_grads(core, back_p, back_r, n_own, n_other, n_up, inputs):
    tokens = inputs.shape[0]
    return pl.pallas_call(
        query_grad_kernel,
        grid=(tokens // TILE,),
        in_specs=[SCALAR] + [rows_of(512)] * 2 + [whole(256, 512)] * 3 + [rows_of(768)],
        out_specs=[rows_of(256)] + [whole(4, 96, 256)] * 2,
        out_shape=[shape((tokens, 256), BF16)] + SHARES,
        scratch_shapes=[pltpu.VMEM((768, 256), F32), pltpu.VMEM((512, 512), BF16)],
        compiler_params=params(),
        cost_estimate=cost(950000000, 5000000),
        name="query_grads",
    )(core, back_p, back_r, n_own, n_other, n_up, inputs)


def back_kernel(core_ref, x_ref, k_ref, v_ref, s_ref, rate_ref, fi_ref, fu_ref, fo_ref, own_ref, other_ref, bu_ref, kg_ref, vg_ref, rate_out, kept_ref, sent_ref, sums, gk, gv, pair, wi_ref, wu_ref, wo_ref):
    in_order(core_ref, own_ref, other_ref, pair)
    wi_ref[...] = rounded(fi_ref[...])
    wu_ref[...] = rounded(fu_ref[...])
    wo_ref[...] = rounded(fo_ref[...])

    key_rows, scaled = k_ref[...], s_ref[...]
    b_in, b_up, b_out = pair[:256, :], bu_ref[...], pair[256:, :]
    pre_in = product(key_rows, wi_ref[...])
    pre_up = product(key_rows, wu_ref[...])
    upstream = times_transpose(scaled, wo_ref[...])
    press_in = product(key_rows, b_in)
    press_up = product(key_rows, b_up)
    back_hid = product(scaled, b_out)
    sigma = sigmoid(pre_in)
    activation = pre_in * sigma
    fall = 1.0 - sigma
    slope = sigma * (1.0 + pre_in * fall)
    curvature = sigma * fall * (2.0 + pre_in * (1.0 - 2.0 * sigma))
    hidden = rounded(activation * pre_up)
    rise = pre_up * slope
    steep = upstream * slope
    grad_in_rows = rounded(upstream * rise)
    grad_up_rows = rounded(upstream * activation)
    back_upstream = rounded(press_in * rise + press_up * activation)
    back_pre_up = rounded(press_in * steep + back_hid * activation)
    back_pre_in = rounded(press_in * upstream * pre_up * curvature + press_up * steep + back_hid * rise)
    both = token_sum(key_rows, jnp.concatenate([back_pre_in, back_pre_up], axis=1))
    put_sums(sums, (both[:, :512], both[:, 512:], token_sum(scaled, back_upstream)))
    back_scaled = times_transpose(hidden, b_out) + product(back_upstream, wo_ref[...])
    scores = jnp.sum(back_scaled * v_ref[...].astype(F32), axis=1, keepdims=True)
    rate_out[...] = jnp.broadcast_to(scores, (rate_ref.shape[1], 128)).T[:1, :]
    value_grad = rounded(column(rate_ref[...]) * back_scaled)
    vg_ref[...] = value_grad
    key_sum = times_transpose(grad_in_rows, b_in) + times_transpose(grad_up_rows, b_up)
    key_sum = key_sum + times_transpose(back_pre_in, wi_ref[...]) + times_transpose(back_pre_up, wu_ref[...])
    key_grad = rounded(key_sum)
    kg_ref[...] = key_grad
    both = token_sum(x_ref[...], jnp.concatenate([key_grad, value_grad], axis=1))
    gk[...] = both[:, :256]
    gv[...] = both[:, 256:]

    core = core_ref[0]
    for a in range(4):
        mine = sums[pl.ds(pl.multiple_of(core * 384 + 96 * a, 96), 96), :]
        theirs = rounded(sums[pl.ds(pl.multiple_of((1 - core) * 384 + 96 * a, 96), 96), :])
        for side in range(2):
            kept_ref[a, 96 * side : 96 * side + 96, :] = mine[:, 256 * side : 256 * side + 256]
            sent_ref[a, 96 * side : 96 * side + 96, :] = theirs[:, 256 * side : 256 * side + 256]
    share_rows(core, gk, kept_ref, sent_ref, 192)
    share_rows(core, gv, kept_ref, sent_ref, 288)


def update_back(core, inputs, key_rows, value_rows, scaled, rates, fast_in, fast_up, fast_out, b_own, b_other, b_up):
    tokens = key_rows.shape[0]
    return pl.pallas_call(
        back_kernel,
        in_specs=[SCALAR] + [IN_VMEM] * 11,
        out_specs=[IN_VMEM] * 5,
        out_shape=[shape((tokens, 256), BF16)] * 2
        + [shape((1, tokens), F32), shape((4, 384, 256), F32), shape((4, 384, 256), BF16)],
        scratch_shapes=[pltpu.VMEM((768, 512), F32), pltpu.VMEM((768, 256), F32), pltpu.VMEM((768, 256), F32), pltpu.VMEM((512, 512), BF16)]
        + [pltpu.VMEM(*w) for w in WEIGHTS],
        compiler_params=params(),
        cost_estimate=cost(5600000000, 10000000),
        name="update_back",
    )(core, inputs, key_rows, value_rows, scaled, rates, fast_in, fast_up, fast_out, b_own, b_other, b_up)


def input_kernel(q_ref, k_ref, v_ref, pq_ref, pk_ref, pv_ref, out_ref):
    total = times_transpose(q_ref[...], pq_ref[...]) + times_transpose(k_ref[...], pk_ref[...])
    out_ref[...] = rounded(total + times_transpose(v_ref[...], pv_ref[...]))


def input_back(query_grad, key_grad, value_grad, proj_query, proj_key, proj_value):
    tokens = query_grad.shape[0]
    return pl.pallas_call(
        input_kernel,
        grid=(tokens // TILE,),
        in_specs=[rows_of(256)] * 3 + [whole(768, 256)] * 3,
        out_specs=rows_of(768),
        out_shape=shape((tokens, 768), BF16),
        compiler_params=params(),
        cost_estimate=cost(1200000000, 4000000),
        name="input_back",
    )(query_grad, key_grad, value_grad, proj_query, proj_key, proj_value)


SHIFTS = (0.0, 0.05, 0.4, 0.9, 0.9)


def shift_of(sweep):
    shift = jnp.float32(SHIFTS[0])
    for index, value in enumerate(SHIFTS[1:]):
        shift = jnp.where(sweep > index, jnp.float32(value), shift)
    return shift


def coefficients(shift):
    return 3.4445 - 4.775 * shift + 2.0315 * shift * shift, -4.775 + 2.0 * 2.0315 * shift, 2.0315


def on_diagonal(value):
    rows = lax.broadcasted_iota(jnp.int32, (256, 256), 0)
    columns = lax.broadcasted_iota(jnp.int32, (256, 256), 1)
    return jnp.where(rows == columns, value, 0.0)


def newton_schulz(current, shift):
    constant, linear, square = coefficients(shift)
    rows = rounded(current)
    excess = times_transpose(rows, rows)
    excess = excess - on_diagonal(shift)
    short = rounded(excess)
    poly = rounded(linear * excess + square * product(short, short))
    return constant * current + product(poly, rows), (rows, short, poly)


def newton_schulz_back(grad, rows, short, poly, shift):
    constant, linear, square = coefficients(shift)
    grad_rows = rounded(grad)
    outer = times_transpose(grad_rows, rows)
    outer = outer + outer.T
    inner = product(rounded(outer), short)
    inner = rounded(linear * outer + square * (inner + inner.T))
    return constant * grad + (product(poly, grad_rows) + product(inner, rows))


def norm_of(matrix):
    return jnp.sqrt(jnp.sum(matrix * matrix))


def two_matrices(core, half_ref, other_ref, middle):
    middle[pl.ds(pl.multiple_of(core * 128, 128), 128), :] = half_ref[pl.ds(pl.multiple_of((1 - core) * 256, 256), 128), :]
    middle[pl.ds(pl.multiple_of((1 - core) * 128, 128), 128), :] = other_ref[...]
    own = half_ref[pl.ds(pl.multiple_of(core * 128, 128), 256), :]
    return [own.astype(F32), middle[...].astype(F32)]


def ortho_kernel(core_ref, half_ref, other_ref, fast_own_ref, fast_up_ref, own_ref, up_ref, x_ref, a_ref, p_ref, middle, current):
    for index, matrix in enumerate(two_matrices(core_ref[0], half_ref, other_ref, middle)):
        current[index] = matrix * (1.0 / (norm_of(matrix) + 1e-07))

    def step(sweep, carry):
        shift = shift_of(sweep)
        results = [newton_schulz(current[index], shift) for index in range(2)]
        for index, (value, kept) in enumerate(results):
            current[index] = value
            for ref, part in zip((x_ref, a_ref, p_ref), kept):
                ref[sweep, index] = part
        return carry

    lax.fori_loop(0, NS_STEPS, step, 0)
    own_ref[...] = rounded(fast_own_ref[...] + current[0])
    up_ref[...] = rounded(fast_up_ref[...] + current[1])


def ortho(core, half, other, fast_own, fast_up):
    return pl.pallas_call(
        ortho_kernel,
        in_specs=[SCALAR] + [IN_VMEM] * 4,
        out_specs=[IN_VMEM] * 5,
        out_shape=[shape((256, 512), BF16)] * 2 + [shape((NS_STEPS, 2, 256, columns), BF16) for columns in (512, 256, 256)],
        scratch_shapes=[pltpu.VMEM((256, 512), BF16), pltpu.VMEM((2, 256, 512), F32)],
        compiler_params=params(),
        cost_estimate=cost(1700000000, 6000000),
        name="ortho",
    )(core, half, other, fast_own, fast_up)


def ortho_back_kernel(core_ref, th_ref, to_ref, half_ref, other_ref, x_ref, a_ref, p_ref, own_ref, up_ref, middle, grads):
    for index, matrix in enumerate(two_matrices(core_ref[0], half_ref, other_ref, middle)):
        grads[index] = matrix

    def step(done, carry):
        sweep = NS_STEPS - 1 - done
        shift = shift_of(sweep)
        results = []
        for index in range(2):
            kept = [ref[sweep, index] for ref in (x_ref, a_ref, p_ref)]
            results.append(newton_schulz_back(grads[index], *kept, shift))
        for index, value in enumerate(results):
            grads[index] = value
        return carry

    lax.fori_loop(0, NS_STEPS, step, 0)
    totals = two_matrices(core_ref[0], th_ref, to_ref, middle)
    for matrix, grad, out_ref in zip(totals, (grads[0], grads[1]), (own_ref, up_ref)):
        norm = norm_of(matrix)
        scale = 1.0 / (norm + 1e-07)
        dot = jnp.sum(grad * matrix)
        out_ref[...] = rounded(grad * scale - matrix * (dot * scale * scale / norm))


def ortho_back(core, totals, adjoint, trail):
    return pl.pallas_call(
        ortho_back_kernel,
        in_specs=[SCALAR] + [IN_VMEM] * 7,
        out_specs=[IN_VMEM] * 2,
        out_shape=[shape((256, 512), BF16)] * 2,
        scratch_shapes=[pltpu.VMEM((256, 512), BF16), pltpu.VMEM((2, 256, 512), F32)],
        compiler_params=params(),
        cost_estimate=cost(2700000000, 6000000),
        name="ortho_back",
    )(core, *totals, *adjoint, *trail)


def pack_kernel(place_ref, kept_ref, in_ref, one_ref, two_ref, three_ref, mine_ref):
    for offset, out_ref in enumerate((mine_ref, one_ref, two_ref, three_ref)):
        at = lax.rem(place_ref[0] + offset, 4)
        out_ref[...] = (kept_ref[at] + in_ref[at].astype(F32)).astype(out_ref.dtype)


def pack(place, kept, received):
    return pl.pallas_call(
        pack_kernel,
        in_specs=[SCALAR] + [IN_VMEM] * 2,
        out_specs=[IN_VMEM] * 4,
        out_shape=[shape(kept.shape[1:], BF16)] * 3 + [shape(kept.shape[1:], F32)],
        compiler_params=params(),
        cost_estimate=cost(1000000, 2000000),
        name="pack",
    )(place, kept, received)


def pack_both_kernel(place_ref, late_ref, late_in_ref, early_ref, early_in_ref, one_ref, two_ref, three_ref, mine_ref):
    for offset, out_ref in enumerate((mine_ref, one_ref, two_ref, three_ref)):
        at = lax.rem(place_ref[0] + offset, 4)
        out_ref[:384, :] = (late_ref[at] + late_in_ref[at].astype(F32)).astype(out_ref.dtype)
        out_ref[384:, :] = (early_ref[at] + early_in_ref[at].astype(F32)).astype(out_ref.dtype)


def pack_both(place, late, late_in, early, early_in):
    return pl.pallas_call(
        pack_both_kernel,
        in_specs=[SCALAR] + [IN_VMEM] * 4,
        out_specs=[IN_VMEM] * 4,
        out_shape=[shape((576, 256), BF16)] * 3 + [shape((576, 256), F32)],
        compiler_params=params(),
        cost_estimate=cost(1000000, 5000000),
        name="pack_both",
    )(place, late, late_in, early, early_in)


def unpack_kernel(second_ref, mine_ref, a_ref, b_ref, c_ref, one_ref, two_ref, three_ref, contrib_ref, own_ref, total):
    total[...] = mine_ref[...] + a_ref[...].astype(F32) + b_ref[...].astype(F32) + c_ref[...].astype(F32)
    contrib = rounded(total[:192, :])
    contrib_ref[...] = contrib
    for offset, out_ref in enumerate((own_ref, one_ref, two_ref, three_ref)):
        at = lax.rem(second_ref[0] + offset, 4) * 24
        shares = [total[pl.ds(pl.multiple_of(192 + 96 * index + at, 8), 24), :] for index in range(4)]
        if offset:
            out_ref[:192, :] = contrib
            for index in (0, 2):
                out_ref[192 + 24 * index : 240 + 24 * index, :] = rounded(jnp.concatenate(shares[index : index + 2], axis=0))
        else:
            for index in range(4):
                out_ref[24 * index : 24 * index + 24, :] = shares[index]


def unpack(second, mine, blocks):
    return pl.pallas_call(
        unpack_kernel,
        in_specs=[SCALAR] + [IN_VMEM] * 4,
        out_specs=[IN_VMEM] * 5,
        out_shape=[shape((288, 256), BF16)] * 3 + [shape((192, 256), BF16), shape((96, 256), F32)],
        scratch_shapes=[pltpu.VMEM((576, 256), F32)],
        compiler_params=params(),
        cost_estimate=cost(1000000, 2000000),
        name="unpack",
    )(second, mine, *blocks)


def finish_kernel(core_ref, half_ref, other_ref, gi_ref, gu_ref, go_ref, scratch):
    core = core_ref[0]
    scratch[pl.ds(pl.multiple_of(core * 384, 384), 384), :] = half_ref[...]
    scratch[pl.ds(pl.multiple_of((1 - core) * 384, 384), 384), :] = other_ref[...]
    gi_ref[...] = scratch[:256, :].astype(F32)
    gu_ref[...] = scratch[256:512, :].astype(F32)
    go_ref[...] = scratch[512:, :].astype(F32).T


def finish(core, half, other):
    return pl.pallas_call(
        finish_kernel,
        in_specs=[SCALAR] + [IN_VMEM] * 2,
        out_specs=[IN_VMEM] * 3,
        out_shape=[shape((256, 512), F32)] * 2 + [shape((512, 256), F32)],
        scratch_shapes=[pltpu.VMEM((768, 512), BF16)],
        compiler_params=params(),
        cost_estimate=cost(1000000, 3000000),
        name="finish",
    )(core, half, other)


def ring_pairs(first, offset):
    pairs = []
    for index in range(32):
        z, x, core = index // 8, (index // 2) % 4, index % 2
        if (core == 0) == first:
            x = (x + offset) % 4
        else:
            z = (z + offset) % 4
        pairs.append((index, z * 8 + x * 2 + core))
    return pairs


def swap_cores(value):
    return lax.ppermute(value, "seq", [(index, index ^ 1) for index in range(32)])


def places():
    me = lax.axis_index("seq")
    z, x, core = me // 8, (me // 2) % 4, me % 2
    return core, jnp.where(core == 0, x, z), jnp.where(core == 0, z, x)


def pick(which, parts):
    return lax.select_n(which, *parts)


def part_at(parts, which):
    return lax.dynamic_index_in_dim(parts, which % 4, 0, keepdims=False)


def scatter_four(parts, place, first):
    received = [
        lax.ppermute(rounded(part_at(parts, place + offset)), "seq", ring_pairs(first, offset)) for offset in (1, 2, 3)
    ]
    total = part_at(parts, place)
    for block in received:
        total = total + block.astype(jnp.float32)
    return total


def exchange_four(block, first):
    return [block] + [lax.ppermute(block, "seq", ring_pairs(first, offset)) for offset in (1, 2, 3)]


def sum_four(blocks):
    a, b, c, d = [block.astype(jnp.float32) for block in blocks]
    return (a + c) + (b + d)


def in_places(blocks, place):
    return jnp.concatenate([pick((place - j) % 4, blocks) for j in range(4)], axis=0)


def middle_half(half, core):
    return swap_cores(jnp.where(core == 0, half[256:], half[:128]))


def together(*values):
    return lax.optimization_barrier(values)


def body(
    inputs,
    token_rates,
    proj_query,
    proj_key,
    proj_value,
    proj_output,
    fast_in,
    fast_up,
    fast_out,
    cotangent,
):
    core_at, place, second = places()
    core = core_at.reshape(1)
    rates = token_rates.reshape(1, -1)

    query_rows, key_rows, value_rows, scaled, kept, sent = update_rows(
        core, inputs, rates, proj_query, proj_key, proj_value, fast_in, fast_up, fast_out
    )
    quarter = scatter_four((kept + swap_cores(sent).astype(F32)).reshape(4, 96, 512), place, True)
    shared = sum_four(exchange_four(rounded(quarter), False))
    back_output, fast_own = back_output_rows(core, together(shared, cotangent)[1], proj_output, fast_in, fast_out)
    blocks, back_output, fast_own = together(exchange_four(rounded(shared), True), back_output, fast_own)
    half = in_places(blocks, place)
    totals = half, middle_half(half, core_at)
    n_own, n_up, *trail = ortho(core, *totals, fast_own, fast_up)
    n_other = swap_cores(n_own)

    back_p, back_r, hidden_q, kept, sent = query_rows_back(core, query_rows, back_output, n_own, n_other, n_up)
    half = (kept + swap_cores(sent).astype(F32)).reshape(4, 96, 512)
    half, hidden_q, back_p, back_r = together(half, hidden_q, back_p, back_r)
    out_kept, out_sent = out_grads(core, hidden_q, n_own, n_other, cotangent)
    quarter, out_kept, out_sent, back_p, back_r = together(scatter_four(half, place, True), out_kept, out_sent, back_p, back_r)
    query_grad, query_kept, query_sent = query_grads(core, back_p, back_r, n_own, n_other, n_up, inputs)
    blocks, query_grad, query_kept, query_sent = together(
        exchange_four(rounded(quarter), False), query_grad, query_kept, query_sent
    )
    adjoint_share = sum_four(blocks)
    blocks = exchange_four(rounded(adjoint_share), True)
    early_sent = jnp.concatenate([query_sent, out_sent], axis=1)
    half = in_places(blocks, place)
    b_own, b_up = ortho_back(core, totals, (half, middle_half(half, core_at)), trail)
    b_other = swap_cores(b_own)
    early = jnp.concatenate([query_kept, out_kept], axis=1)
    early_in = swap_cores(early_sent)

    key_grad, value_grad, back_rate, kept, sent = update_back(
        core, inputs, key_rows, value_rows, scaled, rates, fast_in, fast_up, fast_out, b_own, b_other, b_up
    )
    back_inputs = input_back(query_grad, key_grad, value_grad, proj_query, proj_key, proj_value)
    *blocks, mine = pack_both(place.reshape(1), kept, swap_cores(sent), early, early_in)
    blocks = [lax.ppermute(block, "seq", ring_pairs(True, offset + 1)) for offset, block in enumerate(blocks)]
    *blocks, contrib, mine = unpack(second.reshape(1), mine, blocks)
    received = [lax.ppermute(block, "seq", ring_pairs(False, offset + 1)) for offset, block in enumerate(blocks)]
    summed = sum_four([contrib] + [block[:192] for block in received])
    for block in received:
        mine = mine + block[192:].astype(F32)
    grad_key, grad_value, grad_query, grad_output = [mine[24 * index : 24 * index + 24] for index in range(4)]
    share = adjoint_share + jnp.concatenate([summed[:96], summed[96:]], axis=1)
    blocks = exchange_four(rounded(share), True)
    half = in_places(blocks, place)
    grad_in, grad_up, grad_out = finish(core, half, swap_cores(half))
    return (
        back_inputs,
        back_rate.reshape(-1),
        grad_in,
        grad_up,
        grad_out,
        grad_query,
        grad_key,
        grad_value,
        grad_output.T,
    )


def solution(mesh):
    in_specs = (
        P(("batch", "seq"), None),
        P(("batch", "seq")),
        P(),
        P(),
        P(),
        P(),
        P(),
        P(),
        P(),
        P(("batch", "seq"), None),
    )
    out_specs = (
        P(("batch", "seq"), None),
        P(("batch", "seq")),
        P("batch", None),
        P("batch", None),
        P("batch", None),
        P("seq", "batch"),
        P("seq", "batch"),
        P("seq", "batch"),
        P("batch", "seq"),
    )
    return jax.shard_map(body, mesh=mesh, in_specs=in_specs, out_specs=out_specs, check_vma=False)
```

profile of v0, /device:TPU:1, one launch (start us, length us, event | category | flops | bytes accessed | tf_op | source)
XLA Modules:
  0.0 141.4 jit_solution(8621155579059138347)
XLA Ops:
  0.7 6.9 %update_rows.1 = (bf16[1024,256]{1,0:T(8,128)(2,1)}, bf16[1024,256]{1,0:T(8,128)(2,1)}, bf16[1024,256]{1,0:T(8,128)(2,1)}, bf16[1024,256]{1,0:T(8,128)(2,1)}, f3...) custom-call(s32[1]{0:T(128)} %bitcast.core_ref, bf16[1024,768]{1,0:T(8,128)(2,1)} %x_ref.5, f32[1,1024]{1,0:T(1,128)} %bitcast.35, ...), custom_call_target="tpu_custom_call" | custom-call | flops 2400000000 | bytes 6000000 | tf_op jit(solution)/shard_map/update_rows/pallas_call | solution.py:149
  9.0 1.6 %collective-permute-done = bf16[384,512]{1,0:T(8,128)(2,1)S(1)} collective-permute-done((bf16[384,512]{1,0:T(8,128)(2,1)}, bf16[384,512]{1,0:T(8,128)(2,1)S(1)}, u32[]{:S(2)}, u32[]{:S(2)}) %collective-permute-start) | collective-permute-done | bytes 393248 | tf_op jit(solution)/shard_map/ppermute | solution.py:590
  13.5 1.7 %collective-permute-start.1 = (bf16[96,512]{1,0:T(8,128)(2,1)}, bf16[96,512]{1,0:T(8,128)(2,1)S(1)}, u32[]{:S(2)}, u32[]{:S(2)}) collective-permute-start(bf16[96,512]{1,0:T(8,128)(2,1)} %get-tuple-element.142), channel_id=1, source_target_pairs={{0,8},{4,36},{8,16},{12,44},{16,24},{20,52},{24,0},{28,60},{32,40}... | collective-permute-start | bytes 294920 | tf_op jit(solution)/shard_map/ppermute | solution.py:609
  15.2 2.1 %collective-permute-start.3 = (bf16[96,512]{1,0:T(8,128)(2,1)S(1)}, bf16[96,512]{1,0:T(8,128)(2,1)S(1)}, u32[]{:S(2)}, u32[]{:S(2)}) collective-permute-start(bf16[96,512]{1,0:T(8,128)(2,1)S(1)} %get-tuple-element.143), channel_id=1, source_target_pairs={{0,24},{4,100},{8,0},{12,108},{16,8},{20,116},{24,16},{28,124},{32... | collective-permute-start | bytes 294920 | tf_op jit(solution)/shard_map/ppermute | solution.py:609
  19.6 3.1 %collective-permute-done.2 = bf16[96,512]{1,0:T(8,128)(2,1)S(1)} collective-permute-done((bf16[96,512]{1,0:T(8,128)(2,1)S(1)}, bf16[96,512]{1,0:T(8,128)(2,1)S(1)}, u32[]{:S(2)}, u32[]{:S(2)}) %collective-permute-start.2) | collective-permute-done | bytes 98336 | tf_op jit(solution)/shard_map/ppermute | solution.py:609
  23.6 2.3 %collective-permute-start.6 = (bf16[96,512]{1,0:T(8,128)(2,1)S(1)}, bf16[96,512]{1,0:T(8,128)(2,1)S(1)}, u32[]{:S(2)}, u32[]{:S(2)}) collective-permute-start(bf16[96,512]{1,0:T(8,128)(2,1)S(1)} %fusion.5), channel_id=1, source_target_pairs={{0,96},{4,28},{8,104},{12,4},{16,112},{20,12},{24,120},{28,20},{32... | collective-permute-start | bytes 294920 | tf_op jit(solution)/shard_map/ppermute | solution.py:618
  25.9 1.7 %collective-permute-start.4 = (bf16[96,512]{1,0:T(8,128)(2,1)S(1)}, bf16[96,512]{1,0:T(8,128)(2,1)S(1)}, u32[]{:S(2)}, u32[]{:S(2)}) collective-permute-start(bf16[96,512]{1,0:T(8,128)(2,1)S(1)} %fusion.5), channel_id=1, source_target_pairs={{0,64},{4,20},{8,72},{12,28},{16,80},{20,4},{24,88},{28,12},{32,96... | collective-permute-start | bytes 294920 | tf_op jit(solution)/shard_map/ppermute | solution.py:618
  27.6 4.0 %collective-permute-done.5 = bf16[96,512]{1,0:T(8,128)(2,1)S(1)} collective-permute-done((bf16[96,512]{1,0:T(8,128)(2,1)S(1)}, bf16[96,512]{1,0:T(8,128)(2,1)S(1)}, u32[]{:S(2)}, u32[]{:S(2)}) %collective-permute-start.5) | collective-permute-done | bytes 98336 | tf_op jit(solution)/shard_map/ppermute | solution.py:618
  31.7 1.8 %collective-permute-start.9 = (bf16[96,512]{1,0:T(8,128)(2,1)S(1)}, bf16[96,512]{1,0:T(8,128)(2,1)S(1)}, u32[]{:S(2)}, u32[]{:S(2)}) collective-permute-start(bf16[96,512]{1,0:T(8,128)(2,1)S(1)} %add_add_fusion.2), channel_id=1, source_target_pairs={{0,24},{4,100},{8,0},{12,108},{16,8},{20,116},{24,16},{28,124},{32... | collective-permute-start | bytes 294920 | tf_op jit(solution)/shard_map/ppermute | solution.py:618
  35.5 3.1 %collective-permute-done.8 = bf16[96,512]{1,0:T(8,128)(2,1)S(1)} collective-permute-done((bf16[96,512]{1,0:T(8,128)(2,1)S(1)}, bf16[96,512]{1,0:T(8,128)(2,1)S(1)}, u32[]{:S(2)}, u32[]{:S(2)}) %collective-permute-start.8) | collective-permute-done | bytes 98336 | tf_op jit(solution)/shard_map/ppermute | solution.py:618
  39.6 4.7 %collective-permute-start.10 = (bf16[128,512]{1,0:T(8,128)(2,1)S(1)}, bf16[128,512]{1,0:T(8,128)(2,1)S(1)}, u32[]{:S(2)}, u32[]{:S(2)}) collective-permute-start(bf16[128,512]{1,0:T(8,128)(2,1)S(1)} %fusion.7), channel_id=1, source_target_pairs={{0,4},{4,0},{8,12},{12,8},{16,20},{20,16},{24,28},{28,24},{32,36},... | collective-permute-start | bytes 393224 | tf_op jit(solution)/shard_map/ppermute | solution.py:590
  45.3 5.2 %ortho.1 = (bf16[256,512]{1,0:T(8,128)(2,1)S(1)}, bf16[256,512]{1,0:T(8,128)(2,1)S(1)}, bf16[5,2,256,512]{3,2,1,0:T(8,128)(2,1)S(1)}, bf16[5,2,256,256]{3,2,1,0:T(8,128)(2,1)S(1)}, bf16[5,2,256,256]{3,2,1,0:T(8,128)(2,1)S(1)}) custom-call(s32[1]{0:T(128)} %bitcast.core_ref, bf16[384,512]{1,0:T(8,128)(2,1)S(1)} %pad_maximum_fusion.1.half_ref.th_ref, ...), custom_call_target="tpu_custom_call" | custom-call | flops 1700000000 | bytes 6000000 | tf_op jit(solution)/shard_map/ortho/pallas_call | solution.py:440
  52.3 2.7 %query_rows_back.1 = (bf16[1024,512]{1,0:T(8,128)(2,1)S(1)}, bf16[1024,512]{1,0:T(8,128)(2,1)S(1)}, bf16[1024,512]{1,0:T(8,128)(2,1)S(1)}, f32[384,512]{1,0:T(8,128)S(1)}, bf16[384,512]{1,0:T(8,128)(2,1)S(1)}) custom-call(s32[1]{0:T(128)} %bitcast.core_ref, bf16[1024,256]{1,0:T(8,128)(2,1)S(1)} %copy-done.14, ...), custom_call_target="tpu_custom_call" | custom-call | flops 1600000000 | bytes 6000000 | tf_op jit(solution)/shard_map/query_rows_back/pallas_call | solution.py:208
  57.1 2.7 %collective-permute-start.15 = (bf16[96,512]{1,0:T(8,128)(2,1)S(1)}, bf16[96,512]{1,0:T(8,128)(2,1)S(1)}, u32[]{:S(2)}, u32[]{:S(2)}) collective-permute-start(bf16[96,512]{1,0:T(8,128)(2,1)S(1)} %get-tuple-element.140), channel_id=1, source_target_pairs={{0,24},{4,100},{8,0},{12,108},{16,8},{20,116},{24,16},{28,124},{32... | collective-permute-start | bytes 294920 | tf_op jit(solution)/shard_map/ppermute | solution.py:609
  60.7 1.9 %out_grads.1 = (f32[4,96,256]{2,1,0:T(8,128)S(1)}, bf16[4,96,256]{2,1,0:T(8,128)(2,1)S(1)}) custom-call(s32[1]{0:T(128)} %bitcast.core_ref, bf16[1024,512]{1,0:T(8,128)(2,1)S(1)} %get-tuple-element.94.h_ref, bf16[256,512]{1,0:T(8,128)(2,1)S(1)} %get-tuple-element.86.own_ref, bf16[256,512]{1,0:T(8,128)(2,1)S(1)} %collective-permute-done.11.other_ref, ...), custom_call_target="tpu_custom_call" | custom-call | flops 700000000 | bytes 4000000 | tf_op jit(solution)/shard_map/out_grads/pallas_call | solution.py:239
  62.6 2.1 %collective-permute-done.14 = bf16[96,512]{1,0:T(8,128)(2,1)S(1)} collective-permute-done((bf16[96,512]{1,0:T(8,128)(2,1)S(1)}, bf16[96,512]{1,0:T(8,128)(2,1)S(1)}, u32[]{:S(2)}, u32[]{:S(2)}) %collective-permute-start.14) | collective-permute-done | bytes 98336 | tf_op jit(solution)/shard_map/ppermute | solution.py:609
  66.6 2.4 %query_grads.1 = (bf16[1024,256]{1,0:T(8,128)(2,1)S(1)}, f32[4,96,256]{2,1,0:T(8,128)S(1)}, bf16[4,96,256]{2,1,0:T(8,128)(2,1)S(1)}) custom-call(s32[1]{0:T(128)} %bitcast.core_ref, bf16[1024,512]{1,0:T(8,128)(2,1)S(1)} %get-tuple-element.100.bp_ref, bf16[1024,512]{1,0:T(8,128)(2,1)S(1)} %get-tuple-element.101.br_ref, ...), custom_call_target="tpu_custom_call" | custom-call | flops 950000000 | bytes 5000000 | tf_op jit(solution)/shard_map/query_grads/pallas_call | solution.py:269
  73.5 1.9 %collective-permute-done.21 = bf16[96,512]{1,0:T(8,128)(2,1)S(1)} collective-permute-done((bf16[96,512]{1,0:T(8,128)(2,1)S(1)}, bf16[96,512]{1,0:T(8,128)(2,1)S(1)}, u32[]{:S(2)}, u32[]{:S(2)}) %collective-permute-start.21) | collective-permute-done | bytes 98336 | tf_op jit(solution)/shard_map/ppermute | solution.py:618
  75.4 2.3 %collective-permute-done.20 = bf16[96,512]{1,0:T(8,128)(2,1)S(1)} collective-permute-done((bf16[96,512]{1,0:T(8,128)(2,1)S(1)}, bf16[96,512]{1,0:T(8,128)(2,1)S(1)}, u32[]{:S(2)}, u32[]{:S(2)}) %collective-permute-start.20) | collective-permute-done | bytes 98336 | tf_op jit(solution)/shard_map/ppermute | solution.py:618
  78.7 6.0 %collective-permute-start.22 = (bf16[128,512]{1,0:T(8,128)(2,1)S(1)}, bf16[128,512]{1,0:T(8,128)(2,1)S(1)}, u32[]{:S(2)}, u32[]{:S(2)}) collective-permute-start(bf16[128,512]{1,0:T(8,128)(2,1)S(1)} %fusion.6), channel_id=1, source_target_pairs={{0,4},{4,0},{8,12},{12,8},{16,20},{20,16},{24,28},{28,24},{32,36},... | collective-permute-start | bytes 393224 | tf_op jit(solution)/shard_map/ppermute | solution.py:590
  85.7 6.5 %ortho_back.1 = (bf16[256,512]{1,0:T(8,128)(2,1)S(1)}, bf16[256,512]{1,0:T(8,128)(2,1)S(1)}) custom-call(s32[1]{0:T(128)} %bitcast.core_ref, bf16[384,512]{1,0:T(8,128)(2,1)S(1)} %pad_maximum_fusion.1.half_ref.th_ref, bf16[128,512]{1,0:T(8,128)(2,1)S(1)} %collective-permute-done.10.other_ref.to_ref, bf16[384,512]{1,0:T(8,128)(2,1)S(1)} %pad_maximum_fusion.2.half_ref, ...), custom_call_target="tpu_custom_call" | custom-call | flops 2700000000 | bytes 6000000 | tf_op jit(solution)/shard_map/ortho_back/pallas_call | solution.py:477
  94.1 9.1 %update_back.1 = (bf16[1024,256]{1,0:T(8,128)(2,1)S(1)}, bf16[1024,256]{1,0:T(8,128)(2,1)S(1)}, f32[1,1024]{1,0:T(1,128)}, f32[4,384,256]{2,1,0:T(8,128)S(1)}, bf16[4,384,256]{2,1,0:T(8,128)(2,1)S(1)}) custom-call(s32[1]{0:T(128)} %bitcast.core_ref, bf16[1024,768]{1,0:T(8,128)(2,1)S(1)} %copy-done.1, bf16[1024,256]{1,0:T(8,128)(2,1)S(1)} %copy-done.15, ...), custom_call_target="tpu_custom_call" | custom-call | flops 5600000000 | bytes 10000000 | tf_op jit(solution)/shard_map/update_back/pallas_call | solution.py:337
  105.5 2.2 %collective-permute-done.25.early_in_ref = bf16[4,192,256]{2,1,0:T(8,128)(2,1)S(1)} collective-permute-done((bf16[4,192,256]{2,1,0:T(8,128)(2,1)S(1)}, bf16[4,192,256]{2,1,0:T(8,128)(2,1)S(1)}, u32[]{:S(2)}, u32[]{:S(2)}) %collective-permute-start.25) | collective-permute-done | bytes 393248 | tf_op jit(solution)/shard_map/ppermute | solution.py:590
  107.9 1.8 %collective-permute-start.27 = (bf16[576,256]{1,0:T(8,128)(2,1)S(1)}, bf16[576,256]{1,0:T(8,128)(2,1)S(1)}, u32[]{:S(2)}, u32[]{:S(2)}) collective-permute-start(bf16[576,256]{1,0:T(8,128)(2,1)S(1)} %get-tuple-element.129), channel_id=1, source_target_pairs={{0,16},{4,68},{8,24},{12,76},{16,0},{20,84},{24,8},{28,92},{32,48}... | collective-permute-start | bytes 884744 | tf_op jit(solution)/shard_map/ppermute | solution.py:689
  111.0 7.2 %collective-permute-done.26.a_ref = bf16[576,256]{1,0:T(8,128)(2,1)S(1)} collective-permute-done((bf16[576,256]{1,0:T(8,128)(2,1)S(1)}, bf16[576,256]{1,0:T(8,128)(2,1)S(1)}, u32[]{:S(2)}, u32[]{:S(2)}) %collective-permute-start.26) | collective-permute-done | bytes 294944 | tf_op jit(solution)/shard_map/ppermute | solution.py:689
  120.8 1.7 %collective-permute-start.31 = (bf16[288,256]{1,0:T(8,128)(2,1)S(1)}, bf16[288,256]{1,0:T(8,128)(2,1)S(1)}, u32[]{:S(2)}, u32[]{:S(2)}) collective-permute-start(bf16[288,256]{1,0:T(8,128)(2,1)S(1)} %get-tuple-element.134), channel_id=1, source_target_pairs={{0,96},{4,28},{8,104},{12,4},{16,112},{20,12},{24,120},{28,20},{32... | collective-permute-start | bytes 442376 | tf_op jit(solution)/shard_map/ppermute | solution.py:691
  122.5 2.2 %collective-permute-done.29 = bf16[288,256]{1,0:T(8,128)(2,1)S(1)} collective-permute-done((bf16[288,256]{1,0:T(8,128)(2,1)S(1)}, bf16[288,256]{1,0:T(8,128)(2,1)S(1)}, u32[]{:S(2)}, u32[]{:S(2)}) %collective-permute-start.29) | collective-permute-done | bytes 147488 | tf_op jit(solution)/shard_map/ppermute | solution.py:691
  124.7 1.8 %collective-permute-done.30 = bf16[288,256]{1,0:T(8,128)(2,1)S(1)} collective-permute-done((bf16[288,256]{1,0:T(8,128)(2,1)S(1)}, bf16[288,256]{1,0:T(8,128)(2,1)S(1)}, u32[]{:S(2)}, u32[]{:S(2)}) %collective-permute-start.30) | collective-permute-done | bytes 147488 | tf_op jit(solution)/shard_map/ppermute | solution.py:691
  126.6 1.8 %collective-permute-start.34 = (bf16[96,512]{1,0:T(8,128)(2,1)S(1)}, bf16[96,512]{1,0:T(8,128)(2,1)S(1)}, u32[]{:S(2)}, u32[]{:S(2)}) collective-permute-start(bf16[96,512]{1,0:T(8,128)(2,1)S(1)} %fusion), channel_id=1, source_target_pairs={{0,24},{4,100},{8,0},{12,108},{16,8},{20,116},{24,16},{28,124},{32... | collective-permute-start | bytes 294920 | tf_op jit(solution)/shard_map/ppermute | solution.py:618
  129.2 2.5 %input_back.1 = bf16[1024,768]{1,0:T(8,128)(2,1)} custom-call(bf16[1024,256]{1,0:T(8,128)(2,1)S(1)} %get-tuple-element.105.q_ref, bf16[1024,256]{1,0:T(8,128)(2,1)S(1)} %copy-done.11, bf16[1024,256]{1,0:T(8,128)(2,1)S(1)} %copy-done.13, bf16[768,256]{1,0:T(8,128)(2,1)S(1)} %copy-done.6, bf16[768,256]{1,0:T(8,128)(2,1)S(1)} %copy-done.7, ...), custom_call_target="tpu_custom_call" | custom-call | flops 1200000000 | bytes 4000000 | tf_op jit(solution)/shard_map/input_back/pallas_call | solution.py:358
  131.7 1.8 %collective-permute-done.33 = bf16[96,512]{1,0:T(8,128)(2,1)S(1)} collective-permute-done((bf16[96,512]{1,0:T(8,128)(2,1)S(1)}, bf16[96,512]{1,0:T(8,128)(2,1)S(1)}, u32[]{:S(2)}, u32[]{:S(2)}) %collective-permute-start.33) | collective-permute-done | bytes 98336 | tf_op jit(solution)/shard_map/ppermute | solution.py:618
  134.3 4.5 %collective-permute-start.35 = (bf16[384,512]{1,0:T(8,128)(2,1)S(1)}, bf16[384,512]{1,0:T(8,128)(2,1)S(1)}, u32[]{:S(2)}, u32[]{:S(2)}) collective-permute-start(bf16[384,512]{1,0:T(8,128)(2,1)S(1)} %pad_maximum_fusion.4.half_ref), channel_id=1, source_target_pairs={{0,4},{4,0},{8,12},{12,8},{16,20},{20,16},{24,28},{28,24},{32,36},... | collective-permute-start | bytes 1179656 | tf_op jit(solution)/shard_map/ppermute | solution.py:590
  (113 shorter events, 37.2 us)
Async XLA Ops:
  7.6 3.0 %collective-permute-start = (bf16[384,512]{1,0:T(8,128)(2,1)}, bf16[384,512]{1,0:T(8,128)(2,1)S(1)}, u32[]{:S(2)}, u32[]{:S(2)}) collective-permute-start(bf16[384,512]{1,0:T(8,128)(2,1)} %get-tuple-element.76), channel_id=1, source_target_pairs={{0,4},{4,0},{8,12},{12,8},{16,20},{20,16},{24,28},{28,24},{32,36},... | collective-permute-start | bytes 1179656 | tf_op jit(solution)/shard_map/ppermute | solution.py:590
  13.5 6.1 %collective-permute-start.1 = (bf16[96,512]{1,0:T(8,128)(2,1)}, bf16[96,512]{1,0:T(8,128)(2,1)S(1)}, u32[]{:S(2)}, u32[]{:S(2)}) collective-permute-start(bf16[96,512]{1,0:T(8,128)(2,1)} %get-tuple-element.142), channel_id=1, source_target_pairs={{0,8},{4,36},{8,16},{12,44},{16,24},{20,52},{24,0},{28,60},{32,40}... | collective-permute-start | bytes 294920 | tf_op jit(solution)/shard_map/ppermute | solution.py:609
  15.2 4.3 %collective-permute-start.3 = (bf16[96,512]{1,0:T(8,128)(2,1)S(1)}, bf16[96,512]{1,0:T(8,128)(2,1)S(1)}, u32[]{:S(2)}, u32[]{:S(2)}) collective-permute-start(bf16[96,512]{1,0:T(8,128)(2,1)S(1)} %get-tuple-element.143), channel_id=1, source_target_pairs={{0,24},{4,100},{8,0},{12,108},{16,8},{20,116},{24,16},{28,124},{32... | collective-permute-start | bytes 294920 | tf_op jit(solution)/shard_map/ppermute | solution.py:609
  17.4 5.3 %collective-permute-start.2 = (bf16[96,512]{1,0:T(8,128)(2,1)S(1)}, bf16[96,512]{1,0:T(8,128)(2,1)S(1)}, u32[]{:S(2)}, u32[]{:S(2)}) collective-permute-start(bf16[96,512]{1,0:T(8,128)(2,1)S(1)} %get-tuple-element.144), channel_id=1, source_target_pairs={{0,16},{4,68},{8,24},{12,76},{16,0},{20,84},{24,8},{28,92},{32,48}... | collective-permute-start | bytes 294920 | tf_op jit(solution)/shard_map/ppermute | solution.py:609
  23.6 4.0 %collective-permute-start.6 = (bf16[96,512]{1,0:T(8,128)(2,1)S(1)}, bf16[96,512]{1,0:T(8,128)(2,1)S(1)}, u32[]{:S(2)}, u32[]{:S(2)}) collective-permute-start(bf16[96,512]{1,0:T(8,128)(2,1)S(1)} %fusion.5), channel_id=1, source_target_pairs={{0,96},{4,28},{8,104},{12,4},{16,112},{20,12},{24,120},{28,20},{32... | collective-permute-start | bytes 294920 | tf_op jit(solution)/shard_map/ppermute | solution.py:618
  25.9 5.7 %collective-permute-start.5 = (bf16[96,512]{1,0:T(8,128)(2,1)S(1)}, bf16[96,512]{1,0:T(8,128)(2,1)S(1)}, u32[]{:S(2)}, u32[]{:S(2)}) collective-permute-start(bf16[96,512]{1,0:T(8,128)(2,1)S(1)} %fusion.5), channel_id=1, source_target_pairs={{0,32},{4,12},{8,40},{12,20},{16,48},{20,28},{24,56},{28,4},{32,64... | collective-permute-start | bytes 294920 | tf_op jit(solution)/shard_map/ppermute | solution.py:618
  25.9 5.7 %collective-permute-start.4 = (bf16[96,512]{1,0:T(8,128)(2,1)S(1)}, bf16[96,512]{1,0:T(8,128)(2,1)S(1)}, u32[]{:S(2)}, u32[]{:S(2)}) collective-permute-start(bf16[96,512]{1,0:T(8,128)(2,1)S(1)} %fusion.5), channel_id=1, source_target_pairs={{0,64},{4,20},{8,72},{12,28},{16,80},{20,4},{24,88},{28,12},{32,96... | collective-permute-start | bytes 294920 | tf_op jit(solution)/shard_map/ppermute | solution.py:618
  31.7 3.8 %collective-permute-start.9 = (bf16[96,512]{1,0:T(8,128)(2,1)S(1)}, bf16[96,512]{1,0:T(8,128)(2,1)S(1)}, u32[]{:S(2)}, u32[]{:S(2)}) collective-permute-start(bf16[96,512]{1,0:T(8,128)(2,1)S(1)} %add_add_fusion.2), channel_id=1, source_target_pairs={{0,24},{4,100},{8,0},{12,108},{16,8},{20,116},{24,16},{28,124},{32... | collective-permute-start | bytes 294920 | tf_op jit(solution)/shard_map/ppermute | solution.py:618
  33.5 5.1 %collective-permute-start.8 = (bf16[96,512]{1,0:T(8,128)(2,1)S(1)}, bf16[96,512]{1,0:T(8,128)(2,1)S(1)}, u32[]{:S(2)}, u32[]{:S(2)}) collective-permute-start(bf16[96,512]{1,0:T(8,128)(2,1)S(1)} %add_add_fusion.2), channel_id=1, source_target_pairs={{0,16},{4,68},{8,24},{12,76},{16,0},{20,84},{24,8},{28,92},{32,48}... | collective-permute-start | bytes 294920 | tf_op jit(solution)/shard_map/ppermute | solution.py:618
  33.9 5.6 %collective-permute-start.7 = (bf16[96,512]{1,0:T(8,128)(2,1)S(1)}, bf16[96,512]{1,0:T(8,128)(2,1)S(1)}, u32[]{:S(2)}, u32[]{:S(2)}) collective-permute-start(bf16[96,512]{1,0:T(8,128)(2,1)S(1)} %add_add_fusion.2), channel_id=1, source_target_pairs={{0,8},{4,36},{8,16},{12,44},{16,24},{20,52},{24,0},{28,60},{32,40}... | collective-permute-start | bytes 294920 | tf_op jit(solution)/shard_map/ppermute | solution.py:618
  39.6 5.7 %collective-permute-start.10 = (bf16[128,512]{1,0:T(8,128)(2,1)S(1)}, bf16[128,512]{1,0:T(8,128)(2,1)S(1)}, u32[]{:S(2)}, u32[]{:S(2)}) collective-permute-start(bf16[128,512]{1,0:T(8,128)(2,1)S(1)} %fusion.7), channel_id=1, source_target_pairs={{0,4},{4,0},{8,12},{12,8},{16,20},{20,16},{24,28},{28,24},{32,36},... | collective-permute-start | bytes 393224 | tf_op jit(solution)/shard_map/ppermute | solution.py:590
  57.0 5.6 %collective-permute-start.13 = (bf16[96,512]{1,0:T(8,128)(2,1)S(1)}, bf16[96,512]{1,0:T(8,128)(2,1)S(1)}, u32[]{:S(2)}, u32[]{:S(2)}) collective-permute-start(bf16[96,512]{1,0:T(8,128)(2,1)S(1)} %get-tuple-element.139), channel_id=1, source_target_pairs={{0,8},{4,36},{8,16},{12,44},{16,24},{20,52},{24,0},{28,60},{32,40}... | collective-permute-start | bytes 294920 | tf_op jit(solution)/shard_map/ppermute | solution.py:609
  57.1 5.5 %collective-permute-start.15 = (bf16[96,512]{1,0:T(8,128)(2,1)S(1)}, bf16[96,512]{1,0:T(8,128)(2,1)S(1)}, u32[]{:S(2)}, u32[]{:S(2)}) collective-permute-start(bf16[96,512]{1,0:T(8,128)(2,1)S(1)} %get-tuple-element.140), channel_id=1, source_target_pairs={{0,24},{4,100},{8,0},{12,108},{16,8},{20,116},{24,16},{28,124},{32... | collective-permute-start | bytes 294920 | tf_op jit(solution)/shard_map/ppermute | solution.py:609
  59.7 5.0 %collective-permute-start.14 = (bf16[96,512]{1,0:T(8,128)(2,1)S(1)}, bf16[96,512]{1,0:T(8,128)(2,1)S(1)}, u32[]{:S(2)}, u32[]{:S(2)}) collective-permute-start(bf16[96,512]{1,0:T(8,128)(2,1)S(1)} %get-tuple-element.141), channel_id=1, source_target_pairs={{0,16},{4,68},{8,24},{12,76},{16,0},{20,84},{24,8},{28,92},{32,48}... | collective-permute-start | bytes 294920 | tf_op jit(solution)/shard_map/ppermute | solution.py:609
  64.8 4.2 %collective-permute-start.18 = (bf16[96,512]{1,0:T(8,128)(2,1)S(1)}, bf16[96,512]{1,0:T(8,128)(2,1)S(1)}, u32[]{:S(2)}, u32[]{:S(2)}) collective-permute-start(bf16[96,512]{1,0:T(8,128)(2,1)S(1)} %fusion.2), channel_id=1, source_target_pairs={{0,96},{4,28},{8,104},{12,4},{16,112},{20,12},{24,120},{28,20},{32... | collective-permute-start | bytes 294920 | tf_op jit(solution)/shard_map/ppermute | solution.py:618
  65.5 5.1 %collective-permute-start.17 = (bf16[96,512]{1,0:T(8,128)(2,1)S(1)}, bf16[96,512]{1,0:T(8,128)(2,1)S(1)}, u32[]{:S(2)}, u32[]{:S(2)}) collective-permute-start(bf16[96,512]{1,0:T(8,128)(2,1)S(1)} %fusion.2), channel_id=1, source_target_pairs={{0,64},{4,20},{8,72},{12,28},{16,80},{20,4},{24,88},{28,12},{32,96... | collective-permute-start | bytes 294920 | tf_op jit(solution)/shard_map/ppermute | solution.py:618
  66.0 5.5 %collective-permute-start.16 = (bf16[96,512]{1,0:T(8,128)(2,1)S(1)}, bf16[96,512]{1,0:T(8,128)(2,1)S(1)}, u32[]{:S(2)}, u32[]{:S(2)}) collective-permute-start(bf16[96,512]{1,0:T(8,128)(2,1)S(1)} %fusion.2), channel_id=1, source_target_pairs={{0,32},{4,12},{8,40},{12,20},{16,48},{20,28},{24,56},{28,4},{32,64... | collective-permute-start | bytes 294920 | tf_op jit(solution)/shard_map/ppermute | solution.py:618
  71.5 3.8 %collective-permute-start.21 = (bf16[96,512]{1,0:T(8,128)(2,1)S(1)}, bf16[96,512]{1,0:T(8,128)(2,1)S(1)}, u32[]{:S(2)}, u32[]{:S(2)}) collective-permute-start(bf16[96,512]{1,0:T(8,128)(2,1)S(1)} %fusion.14), channel_id=1, source_target_pairs={{0,24},{4,100},{8,0},{12,108},{16,8},{20,116},{24,16},{28,124},{32... | collective-permute-start | bytes 294920 | tf_op jit(solution)/shard_map/ppermute | solution.py:618
  72.6 5.0 %collective-permute-start.20 = (bf16[96,512]{1,0:T(8,128)(2,1)S(1)}, bf16[96,512]{1,0:T(8,128)(2,1)S(1)}, u32[]{:S(2)}, u32[]{:S(2)}) collective-permute-start(bf16[96,512]{1,0:T(8,128)(2,1)S(1)} %fusion.14), channel_id=1, source_target_pairs={{0,16},{4,68},{8,24},{12,76},{16,0},{20,84},{24,8},{28,92},{32,48}... | collective-permute-start | bytes 294920 | tf_op jit(solution)/shard_map/ppermute | solution.py:618
  73.4 5.3 %collective-permute-start.19 = (bf16[96,512]{1,0:T(8,128)(2,1)S(1)}, bf16[96,512]{1,0:T(8,128)(2,1)S(1)}, u32[]{:S(2)}, u32[]{:S(2)}) collective-permute-start(bf16[96,512]{1,0:T(8,128)(2,1)S(1)} %fusion.14), channel_id=1, source_target_pairs={{0,8},{4,36},{8,16},{12,44},{16,24},{20,52},{24,0},{28,60},{32,40}... | collective-permute-start | bytes 294920 | tf_op jit(solution)/shard_map/ppermute | solution.py:618
  78.7 7.0 %collective-permute-start.22 = (bf16[128,512]{1,0:T(8,128)(2,1)S(1)}, bf16[128,512]{1,0:T(8,128)(2,1)S(1)}, u32[]{:S(2)}, u32[]{:S(2)}) collective-permute-start(bf16[128,512]{1,0:T(8,128)(2,1)S(1)} %fusion.6), channel_id=1, source_target_pairs={{0,4},{4,0},{8,12},{12,8},{16,20},{20,16},{24,28},{28,24},{32,36},... | collective-permute-start | bytes 393224 | tf_op jit(solution)/shard_map/ppermute | solution.py:590
  104.8 2.9 %collective-permute-start.24 = (bf16[4,384,256]{2,1,0:T(8,128)(2,1)S(1)}, bf16[4,384,256]{2,1,0:T(8,128)(2,1)S(1)}, u32[]{:S(2)}, u32[]{:S(2)}) collective-permute-start(bf16[4,384,256]{2,1,0:T(8,128)(2,1)S(1)} %get-tuple-element.122), channel_id=1, source_target_pairs={{0,4},{4,0},{8,12},{12,8},{16,20},{20,16},{24,28},{28,24},{32,36},... | collective-permute-start | bytes 2359304 | tf_op jit(solution)/shard_map/ppermute | solution.py:590
  107.8 10.3 %collective-permute-start.26 = (bf16[576,256]{1,0:T(8,128)(2,1)S(1)}, bf16[576,256]{1,0:T(8,128)(2,1)S(1)}, u32[]{:S(2)}, u32[]{:S(2)}) collective-permute-start(bf16[576,256]{1,0:T(8,128)(2,1)S(1)} %get-tuple-element.128), channel_id=1, source_target_pairs={{0,8},{4,36},{8,16},{12,44},{16,24},{20,52},{24,0},{28,60},{32,40}... | collective-permute-start | bytes 884744 | tf_op jit(solution)/shard_map/ppermute | solution.py:689
  107.9 10.2 %collective-permute-start.27 = (bf16[576,256]{1,0:T(8,128)(2,1)S(1)}, bf16[576,256]{1,0:T(8,128)(2,1)S(1)}, u32[]{:S(2)}, u32[]{:S(2)}) collective-permute-start(bf16[576,256]{1,0:T(8,128)(2,1)S(1)} %get-tuple-element.129), channel_id=1, source_target_pairs={{0,16},{4,68},{8,24},{12,76},{16,0},{20,84},{24,8},{28,92},{32,48}... | collective-permute-start | bytes 884744 | tf_op jit(solution)/shard_map/ppermute | solution.py:689
  109.7 9.1 %collective-permute-start.28 = (bf16[576,256]{1,0:T(8,128)(2,1)S(1)}, bf16[576,256]{1,0:T(8,128)(2,1)S(1)}, u32[]{:S(2)}, u32[]{:S(2)}) collective-permute-start(bf16[576,256]{1,0:T(8,128)(2,1)S(1)} %get-tuple-element.130), channel_id=1, source_target_pairs={{0,24},{4,100},{8,0},{12,108},{16,8},{20,116},{24,16},{28,124},{32... | collective-permute-start | bytes 884744 | tf_op jit(solution)/shard_map/ppermute | solution.py:689
  119.0 5.7 %collective-permute-start.29 = (bf16[288,256]{1,0:T(8,128)(2,1)S(1)}, bf16[288,256]{1,0:T(8,128)(2,1)S(1)}, u32[]{:S(2)}, u32[]{:S(2)}) collective-permute-start(bf16[288,256]{1,0:T(8,128)(2,1)S(1)} %get-tuple-element.132), channel_id=1, source_target_pairs={{0,64},{4,20},{8,72},{12,28},{16,80},{20,4},{24,88},{28,12},{32,96... | collective-permute-start | bytes 442376 | tf_op jit(solution)/shard_map/ppermute | solution.py:691
  119.8 6.7 %collective-permute-start.30 = (bf16[288,256]{1,0:T(8,128)(2,1)S(1)}, bf16[288,256]{1,0:T(8,128)(2,1)S(1)}, u32[]{:S(2)}, u32[]{:S(2)}) collective-permute-start(bf16[288,256]{1,0:T(8,128)(2,1)S(1)} %get-tuple-element.133), channel_id=1, source_target_pairs={{0,32},{4,12},{8,40},{12,20},{16,48},{20,28},{24,56},{28,4},{32,64... | collective-permute-start | bytes 442376 | tf_op jit(solution)/shard_map/ppermute | solution.py:691
  120.8 5.7 %collective-permute-start.31 = (bf16[288,256]{1,0:T(8,128)(2,1)S(1)}, bf16[288,256]{1,0:T(8,128)(2,1)S(1)}, u32[]{:S(2)}, u32[]{:S(2)}) collective-permute-start(bf16[288,256]{1,0:T(8,128)(2,1)S(1)} %get-tuple-element.134), channel_id=1, source_target_pairs={{0,96},{4,28},{8,104},{12,4},{16,112},{20,12},{24,120},{28,20},{32... | collective-permute-start | bytes 442376 | tf_op jit(solution)/shard_map/ppermute | solution.py:691
  126.6 5.1 %collective-permute-start.34 = (bf16[96,512]{1,0:T(8,128)(2,1)S(1)}, bf16[96,512]{1,0:T(8,128)(2,1)S(1)}, u32[]{:S(2)}, u32[]{:S(2)}) collective-permute-start(bf16[96,512]{1,0:T(8,128)(2,1)S(1)} %fusion), channel_id=1, source_target_pairs={{0,24},{4,100},{8,0},{12,108},{16,8},{20,116},{24,16},{28,124},{32... | collective-permute-start | bytes 294920 | tf_op jit(solution)/shard_map/ppermute | solution.py:618
  128.5 5.1 %collective-permute-start.33 = (bf16[96,512]{1,0:T(8,128)(2,1)S(1)}, bf16[96,512]{1,0:T(8,128)(2,1)S(1)}, u32[]{:S(2)}, u32[]{:S(2)}) collective-permute-start(bf16[96,512]{1,0:T(8,128)(2,1)S(1)} %fusion), channel_id=1, source_target_pairs={{0,16},{4,68},{8,24},{12,76},{16,0},{20,84},{24,8},{28,92},{32,48}... | collective-permute-start | bytes 294920 | tf_op jit(solution)/shard_map/ppermute | solution.py:618
  128.5 5.7 %collective-permute-start.32 = (bf16[96,512]{1,0:T(8,128)(2,1)S(1)}, bf16[96,512]{1,0:T(8,128)(2,1)S(1)}, u32[]{:S(2)}, u32[]{:S(2)}) collective-permute-start(bf16[96,512]{1,0:T(8,128)(2,1)S(1)} %fusion), channel_id=1, source_target_pairs={{0,8},{4,36},{8,16},{12,44},{16,24},{20,52},{24,0},{28,60},{32,40}... | collective-permute-start | bytes 294920 | tf_op jit(solution)/shard_map/ppermute | solution.py:618
  134.3 5.8 %collective-permute-start.35 = (bf16[384,512]{1,0:T(8,128)(2,1)S(1)}, bf16[384,512]{1,0:T(8,128)(2,1)S(1)}, u32[]{:S(2)}, u32[]{:S(2)}) collective-permute-start(bf16[384,512]{1,0:T(8,128)(2,1)S(1)} %pad_maximum_fusion.4.half_ref), channel_id=1, source_target_pairs={{0,4},{4,0},{8,12},{12,8},{16,20},{20,16},{24,28},{28,24},{32,36},... | collective-permute-start | bytes 1179656 | tf_op jit(solution)/shard_map/ppermute | solution.py:590
  (23 other events, 215.2 us)
where the time goes:
time: 142 us; the launch traced here: 141 us
  starting transfers between devices  47 us (33%)
  waiting for transfers between devices  46.3 us (33%)
  Pallas kernels  40.1 us (28%)
  local copies, waits for them, and re-layouts  3.91 us (3%)
  other arithmetic  3.16 us (2%)
    ppermute x9, starting transfers between devices, swap_cores(): lax.ppermute(value, 'seq', [(index, index ^ 1) for index in range(32)])  18.9 us
    ppermute x15, waiting for transfers between devices, exchange_four(): lax.ppermute(block, 'seq', ring_pairs(first, offset))  18.4 us
    ppermute x15, starting transfers between devices, exchange_four(): lax.ppermute(block, 'seq', ring_pairs(first, offset))  12.7 us
    ppermute x9, waiting for transfers between devices, swap_cores(): lax.ppermute(value, 'seq', [(index, index ^ 1) for index in range(32)])  10 us
    pallas_call x1, Pallas kernels, update_back(): pl.pallas_call(back_kernel, in_specs=[SCALAR] + [IN_VMEM] * 11, out_specs...  9.08 us
    ppermute x6, starting transfers between devices, scatter_four(): lax.ppermute(rounded(part_at(parts, place + offset)), 'seq', ring_pairs(f...  8.79 us
    ppermute x3, waiting for transfers between devices, body(): lax.ppermute(block, 'seq', ring_pairs(True, offset + 1))  7.81 us
    pallas_call x1, Pallas kernels, update_rows(): pl.pallas_call(update_kernel, grid=(tokens // LARGE,), in_specs=[SCALAR,...  6.92 us
  transfers between devices with their start and end apart: 36, of which 26 were waited for; matrix products, arithmetic and copies ran while one was open for 1% of the time, Pallas kernels for 6%

commit v1 on v0

--- a/solution.py
+++ b/solution.py
@@ -685,7 +685,8 @@
         core, inputs, key_rows, value_rows, scaled, rates, fast_in, fast_up, fast_out, b_own, b_other, b_up
     )
     back_inputs = input_back(query_grad, key_grad, value_grad, proj_query, proj_key, proj_value)
-    *blocks, mine = pack_both(place.reshape(1), kept, swap_cores(sent), early, early_in)
+    place_at, back_inputs = together(place.reshape(1), back_inputs)
+    *blocks, mine = pack_both(place_at, kept, swap_cores(sent), early, early_in)
     blocks = [lax.ppermute(block, "seq", ring_pairs(True, offset + 1)) for offset, block in enumerate(blocks)]
     *blocks, contrib, mine = unpack(second.reshape(1), mine, blocks)
     received = [lax.ppermute(block, "seq", ring_pairs(False, offset + 1)) for offset, block in enumerate(blocks)]

time: 142 us -> 141 us (level)
    ppermute x15, waiting for transfers between devices: 18.4 us -> 21 us  [exchange_four(): lax.ppermute(block, 'seq', ring_pairs(first, offset))]
    ppermute x9, waiting for transfers between devices: 10 us -> 7.85 us  [swap_cores(): lax.ppermute(value, 'seq', [(index, index ^ 1) for index in range(32)])]
where the time goes in v1:
time: 141 us
  starting transfers between devices  47 us (33%)
  waiting for transfers between devices  46.7 us (33%)
  Pallas kernels  40 us (28%)
  other arithmetic  3.15 us (2%)
  local copies, waits for them, and re-layouts  2.84 us (2%)
    ppermute x15, waiting for transfers between devices, exchange_four(): lax.ppermute(block, 'seq', ring_pairs(first, offset))  21 us
    ppermute x9, starting transfers between devices, swap_cores(): lax.ppermute(value, 'seq', [(index, index ^ 1) for index in range(32)])  18.9 us
    ppermute x15, starting transfers between devices, exchange_four(): lax.ppermute(block, 'seq', ring_pairs(first, offset))  12.7 us
    pallas_call x1, Pallas kernels, update_back(): pl.pallas_call(back_kernel, in_specs=[SCALAR] + [IN_VMEM] * 11, out_specs...  9.08 us
    ppermute x6, starting transfers between devices, scatter_four(): lax.ppermute(rounded(part_at(parts, place + offset)), 'seq', ring_pairs(f...  8.8 us
    ppermute x9, waiting for transfers between devices, swap_cores(): lax.ppermute(value, 'seq', [(index, index ^ 1) for index in range(32)])  7.85 us
    ppermute x3, waiting for transfers between devices, body(): lax.ppermute(block, 'seq', ring_pairs(True, offset + 1))  7.8 us
    pallas_call x1, Pallas kernels, update_rows(): pl.pallas_call(update_kernel, grid=(tokens // LARGE,), in_specs=[SCALAR,...  6.91 us
  transfers between devices with their start and end apart: 36, of which 26 were waited for; matrix products, arithmetic and copies ran while one was open for 1% of the time, Pallas kernels for 6%

profile of v1, /device:TPU:1, one launch (start us, length us, event | category | flops | bytes accessed | tf_op | source)
XLA Modules:
  0.0 140.7 jit_solution(4971186590160654969)
XLA Ops:
  0.7 6.9 %update_rows.1 = (bf16[1024,256]{1,0:T(8,128)(2,1)}, bf16[1024,256]{1,0:T(8,128)(2,1)}, bf16[1024,256]{1,0:T(8,128)(2,1)}, bf16[1024,256]{1,0:T(8,128)(2,1)}, f3...) custom-call(s32[1]{0:T(128)} %bitcast.1.core_ref, bf16[1024,768]{1,0:T(8,128)(2,1)} %x_ref.5, f32[1,1024]{1,0:T(1,128)} %bitcast.35, ...), custom_call_target="tpu_custom_call" | custom-call | flops 2400000000 | bytes 6000000 | tf_op jit(solution)/shard_map/update_rows/pallas_call | solution.py:149
  9.0 1.6 %collective-permute-done = bf16[384,512]{1,0:T(8,128)(2,1)S(1)} collective-permute-done((bf16[384,512]{1,0:T(8,128)(2,1)}, bf16[384,512]{1,0:T(8,128)(2,1)S(1)}, u32[]{:S(2)}, u32[]{:S(2)}) %collective-permute-start) | collective-permute-done | bytes 393248 | tf_op jit(solution)/shard_map/ppermute | solution.py:590
  13.5 1.7 %collective-permute-start.1 = (bf16[96,512]{1,0:T(8,128)(2,1)}, bf16[96,512]{1,0:T(8,128)(2,1)S(1)}, u32[]{:S(2)}, u32[]{:S(2)}) collective-permute-start(bf16[96,512]{1,0:T(8,128)(2,1)} %get-tuple-element.146), channel_id=1, source_target_pairs={{0,8},{4,36},{8,16},{12,44},{16,24},{20,52},{24,0},{28,60},{32,40}... | collective-permute-start | bytes 294920 | tf_op jit(solution)/shard_map/ppermute | solution.py:609
  15.2 2.1 %collective-permute-start.3 = (bf16[96,512]{1,0:T(8,128)(2,1)S(1)}, bf16[96,512]{1,0:T(8,128)(2,1)S(1)}, u32[]{:S(2)}, u32[]{:S(2)}) collective-permute-start(bf16[96,512]{1,0:T(8,128)(2,1)S(1)} %get-tuple-element.147), channel_id=1, source_target_pairs={{0,24},{4,100},{8,0},{12,108},{16,8},{20,116},{24,16},{28,124},{32... | collective-permute-start | bytes 294920 | tf_op jit(solution)/shard_map/ppermute | solution.py:609
  19.6 3.1 %collective-permute-done.2 = bf16[96,512]{1,0:T(8,128)(2,1)S(1)} collective-permute-done((bf16[96,512]{1,0:T(8,128)(2,1)S(1)}, bf16[96,512]{1,0:T(8,128)(2,1)S(1)}, u32[]{:S(2)}, u32[]{:S(2)}) %collective-permute-start.2) | collective-permute-done | bytes 98336 | tf_op jit(solution)/shard_map/ppermute | solution.py:609
  23.6 2.3 %collective-permute-start.6 = (bf16[96,512]{1,0:T(8,128)(2,1)S(1)}, bf16[96,512]{1,0:T(8,128)(2,1)S(1)}, u32[]{:S(2)}, u32[]{:S(2)}) collective-permute-start(bf16[96,512]{1,0:T(8,128)(2,1)S(1)} %fusion.5), channel_id=1, source_target_pairs={{0,96},{4,28},{8,104},{12,4},{16,112},{20,12},{24,120},{28,20},{32... | collective-permute-start | bytes 294920 | tf_op jit(solution)/shard_map/ppermute | solution.py:618
  25.9 1.7 %collective-permute-start.4 = (bf16[96,512]{1,0:T(8,128)(2,1)S(1)}, bf16[96,512]{1,0:T(8,128)(2,1)S(1)}, u32[]{:S(2)}, u32[]{:S(2)}) collective-permute-start(bf16[96,512]{1,0:T(8,128)(2,1)S(1)} %fusion.5), channel_id=1, source_target_pairs={{0,64},{4,20},{8,72},{12,28},{16,80},{20,4},{24,88},{28,12},{32,96... | collective-permute-start | bytes 294920 | tf_op jit(solution)/shard_map/ppermute | solution.py:618
  27.6 4.0 %collective-permute-done.5 = bf16[96,512]{1,0:T(8,128)(2,1)S(1)} collective-permute-done((bf16[96,512]{1,0:T(8,128)(2,1)S(1)}, bf16[96,512]{1,0:T(8,128)(2,1)S(1)}, u32[]{:S(2)}, u32[]{:S(2)}) %collective-permute-start.5) | collective-permute-done | bytes 98336 | tf_op jit(solution)/shard_map/ppermute | solution.py:618
  31.6 1.8 %collective-permute-start.9 = (bf16[96,512]{1,0:T(8,128)(2,1)S(1)}, bf16[96,512]{1,0:T(8,128)(2,1)S(1)}, u32[]{:S(2)}, u32[]{:S(2)}) collective-permute-start(bf16[96,512]{1,0:T(8,128)(2,1)S(1)} %add_add_fusion.2), channel_id=1, source_target_pairs={{0,24},{4,100},{8,0},{12,108},{16,8},{20,116},{24,16},{28,124},{32... | collective-permute-start | bytes 294920 | tf_op jit(solution)/shard_map/ppermute | solution.py:618
  35.5 3.1 %collective-permute-done.8 = bf16[96,512]{1,0:T(8,128)(2,1)S(1)} collective-permute-done((bf16[96,512]{1,0:T(8,128)(2,1)S(1)}, bf16[96,512]{1,0:T(8,128)(2,1)S(1)}, u32[]{:S(2)}, u32[]{:S(2)}) %collective-permute-start.8) | collective-permute-done | bytes 98336 | tf_op jit(solution)/shard_map/ppermute | solution.py:618
  39.6 4.7 %collective-permute-start.10 = (bf16[128,512]{1,0:T(8,128)(2,1)S(1)}, bf16[128,512]{1,0:T(8,128)(2,1)S(1)}, u32[]{:S(2)}, u32[]{:S(2)}) collective-permute-start(bf16[128,512]{1,0:T(8,128)(2,1)S(1)} %fusion.7), channel_id=1, source_target_pairs={{0,4},{4,0},{8,12},{12,8},{16,20},{20,16},{24,28},{28,24},{32,36},... | collective-permute-start | bytes 393224 | tf_op jit(solution)/shard_map/ppermute | solution.py:590
  45.3 5.2 %ortho.1 = (bf16[256,512]{1,0:T(8,128)(2,1)S(1)}, bf16[256,512]{1,0:T(8,128)(2,1)S(1)}, bf16[5,2,256,512]{3,2,1,0:T(8,128)(2,1)S(1)}, bf16[5,2,256,256]{3,2,1,0:T(8,128)(2,1)S(1)}, bf16[5,2,256,256]{3,2,1,0:T(8,128)(2,1)S(1)}) custom-call(s32[1]{0:T(128)} %bitcast.1.core_ref, bf16[384,512]{1,0:T(8,128)(2,1)S(1)} %pad_maximum_fusion.1.half_ref.th_ref, ...), custom_call_target="tpu_custom_call" | custom-call | flops 1700000000 | bytes 6000000 | tf_op jit(solution)/shard_map/ortho/pallas_call | solution.py:440
  52.3 2.7 %query_rows_back.1 = (bf16[1024,512]{1,0:T(8,128)(2,1)S(1)}, bf16[1024,512]{1,0:T(8,128)(2,1)S(1)}, bf16[1024,512]{1,0:T(8,128)(2,1)S(1)}, f32[384,512]{1,0:T(8,128)S(1)}, bf16[384,512]{1,0:T(8,128)(2,1)S(1)}) custom-call(s32[1]{0:T(128)} %bitcast.1.core_ref, bf16[1024,256]{1,0:T(8,128)(2,1)S(1)} %copy-done.10, ...), custom_call_target="tpu_custom_call" | custom-call | flops 1600000000 | bytes 6000000 | tf_op jit(solution)/shard_map/query_rows_back/pallas_call | solution.py:208
  57.1 2.7 %collective-permute-start.15 = (bf16[96,512]{1,0:T(8,128)(2,1)S(1)}, bf16[96,512]{1,0:T(8,128)(2,1)S(1)}, u32[]{:S(2)}, u32[]{:S(2)}) collective-permute-start(bf16[96,512]{1,0:T(8,128)(2,1)S(1)} %get-tuple-element.144), channel_id=1, source_target_pairs={{0,24},{4,100},{8,0},{12,108},{16,8},{20,116},{24,16},{28,124},{32... | collective-permute-start | bytes 294920 | tf_op jit(solution)/shard_map/ppermute | solution.py:609
  60.6 1.9 %out_grads.1 = (f32[4,96,256]{2,1,0:T(8,128)S(1)}, bf16[4,96,256]{2,1,0:T(8,128)(2,1)S(1)}) custom-call(s32[1]{0:T(128)} %bitcast.1.core_ref, bf16[1024,512]{1,0:T(8,128)(2,1)S(1)} %get-tuple-element.96.h_ref, bf16[256,512]{1,0:T(8,128)(2,1)S(1)} %get-tuple-element.88.own_ref, bf16[256,512]{1,0:T(8,128)(2,1)S(1)} %collective-permute-done.11.other_ref, ...), custom_call_target="tpu_custom_call" | custom-call | flops 700000000 | bytes 4000000 | tf_op jit(solution)/shard_map/out_grads/pallas_call | solution.py:239
  62.6 2.1 %collective-permute-done.14 = bf16[96,512]{1,0:T(8,128)(2,1)S(1)} collective-permute-done((bf16[96,512]{1,0:T(8,128)(2,1)S(1)}, bf16[96,512]{1,0:T(8,128)(2,1)S(1)}, u32[]{:S(2)}, u32[]{:S(2)}) %collective-permute-start.14) | collective-permute-done | bytes 98336 | tf_op jit(solution)/shard_map/ppermute | solution.py:609
  66.6 2.4 %query_grads.1 = (bf16[1024,256]{1,0:T(8,128)(2,1)S(1)}, f32[4,96,256]{2,1,0:T(8,128)S(1)}, bf16[4,96,256]{2,1,0:T(8,128)(2,1)S(1)}) custom-call(s32[1]{0:T(128)} %bitcast.1.core_ref, bf16[1024,512]{1,0:T(8,128)(2,1)S(1)} %get-tuple-element.102.bp_ref, bf16[1024,512]{1,0:T(8,128)(2,1)S(1)} %get-tuple-element.103.br_ref, ...), custom_call_target="tpu_custom_call" | custom-call | flops 950000000 | bytes 5000000 | tf_op jit(solution)/shard_map/query_grads/pallas_call | solution.py:269
  73.5 1.9 %collective-permute-done.21 = bf16[96,512]{1,0:T(8,128)(2,1)S(1)} collective-permute-done((bf16[96,512]{1,0:T(8,128)(2,1)S(1)}, bf16[96,512]{1,0:T(8,128)(2,1)S(1)}, u32[]{:S(2)}, u32[]{:S(2)}) %collective-permute-start.21) | collective-permute-done | bytes 98336 | tf_op jit(solution)/shard_map/ppermute | solution.py:618
  75.3 2.3 %collective-permute-done.20 = bf16[96,512]{1,0:T(8,128)(2,1)S(1)} collective-permute-done((bf16[96,512]{1,0:T(8,128)(2,1)S(1)}, bf16[96,512]{1,0:T(8,128)(2,1)S(1)}, u32[]{:S(2)}, u32[]{:S(2)}) %collective-permute-start.20) | collective-permute-done | bytes 98336 | tf_op jit(solution)/shard_map/ppermute | solution.py:618
  78.7 6.0 %collective-permute-start.22 = (bf16[128,512]{1,0:T(8,128)(2,1)S(1)}, bf16[128,512]{1,0:T(8,128)(2,1)S(1)}, u32[]{:S(2)}, u32[]{:S(2)}) collective-permute-start(bf16[128,512]{1,0:T(8,128)(2,1)S(1)} %fusion.6), channel_id=1, source_target_pairs={{0,4},{4,0},{8,12},{12,8},{16,20},{20,16},{24,28},{28,24},{32,36},... | collective-permute-start | bytes 393224 | tf_op jit(solution)/shard_map/ppermute | solution.py:590
  85.7 6.5 %ortho_back.1 = (bf16[256,512]{1,0:T(8,128)(2,1)S(1)}, bf16[256,512]{1,0:T(8,128)(2,1)S(1)}) custom-call(s32[1]{0:T(128)} %bitcast.1.core_ref, bf16[384,512]{1,0:T(8,128)(2,1)S(1)} %pad_maximum_fusion.1.half_ref.th_ref, bf16[128,512]{1,0:T(8,128)(2,1)S(1)} %collective-permute-done.10.other_ref.to_ref, bf16[384,512]{1,0:T(8,128)(2,1)S(1)} %pad_maximum_fusion.2.half_ref, ...), custom_call_target="tpu_custom_call" | custom-call | flops 2700000000 | bytes 6000000 | tf_op jit(solution)/shard_map/ortho_back/pallas_call | solution.py:477
  94.1 9.1 %update_back.1 = (bf16[1024,256]{1,0:T(8,128)(2,1)S(1)}, bf16[1024,256]{1,0:T(8,128)(2,1)S(1)}, f32[1,1024]{1,0:T(1,128)}, f32[4,384,256]{2,1,0:T(8,128)S(1)}, bf16[4,384,256]{2,1,0:T(8,128)(2,1)S(1)}) custom-call(s32[1]{0:T(128)} %bitcast.1.core_ref, bf16[1024,768]{1,0:T(8,128)(2,1)S(1)} %copy-done.1, bf16[1024,256]{1,0:T(8,128)(2,1)S(1)} %copy-done.11, ...), custom_call_target="tpu_custom_call" | custom-call | flops 5600000000 | bytes 10000000 | tf_op jit(solution)/shard_map/update_back/pallas_call | solution.py:337
  104.4 2.5 %input_back.1 = bf16[1024,768]{1,0:T(8,128)(2,1)} custom-call(bf16[1024,256]{1,0:T(8,128)(2,1)S(1)} %get-tuple-element.107.q_ref, bf16[1024,256]{1,0:T(8,128)(2,1)S(1)} %get-tuple-element.120.k_ref, bf16[1024,256]{1,0:T(8,128)(2,1)S(1)} %get-tuple-element.121.v_ref, bf16[768,256]{1,0:T(8,128)(2,1)S(1)} %copy-done.6, bf16[768,256]{1,0:T(8,128)(2,1)S(1)} %copy-done.7, ...), custom_call_target="tpu_custom_call" | custom-call | flops 1200000000 | bytes 4000000 | tf_op jit(solution)/shard_map/input_back/pallas_call | solution.py:358
  107.2 1.8 %collective-permute-start.27 = (bf16[576,256]{1,0:T(8,128)(2,1)S(1)}, bf16[576,256]{1,0:T(8,128)(2,1)S(1)}, u32[]{:S(2)}, u32[]{:S(2)}) collective-permute-start(bf16[576,256]{1,0:T(8,128)(2,1)S(1)} %get-tuple-element.133), channel_id=1, source_target_pairs={{0,16},{4,68},{8,24},{12,76},{16,0},{20,84},{24,8},{28,92},{32,48}... | collective-permute-start | bytes 884744 | tf_op jit(solution)/shard_map/ppermute | solution.py:690
  110.3 7.2 %collective-permute-done.26.a_ref = bf16[576,256]{1,0:T(8,128)(2,1)S(1)} collective-permute-done((bf16[576,256]{1,0:T(8,128)(2,1)S(1)}, bf16[576,256]{1,0:T(8,128)(2,1)S(1)}, u32[]{:S(2)}, u32[]{:S(2)}) %collective-permute-start.26) | collective-permute-done | bytes 294944 | tf_op jit(solution)/shard_map/ppermute | solution.py:690
  120.1 1.7 %collective-permute-start.31 = (bf16[288,256]{1,0:T(8,128)(2,1)S(1)}, bf16[288,256]{1,0:T(8,128)(2,1)S(1)}, u32[]{:S(2)}, u32[]{:S(2)}) collective-permute-start(bf16[288,256]{1,0:T(8,128)(2,1)S(1)} %get-tuple-element.138), channel_id=1, source_target_pairs={{0,96},{4,28},{8,104},{12,4},{16,112},{20,12},{24,120},{28,20},{32... | collective-permute-start | bytes 442376 | tf_op jit(solution)/shard_map/ppermute | solution.py:692
  121.8 2.2 %collective-permute-done.29 = bf16[288,256]{1,0:T(8,128)(2,1)S(1)} collective-permute-done((bf16[288,256]{1,0:T(8,128)(2,1)S(1)}, bf16[288,256]{1,0:T(8,128)(2,1)S(1)}, u32[]{:S(2)}, u32[]{:S(2)}) %collective-permute-start.29) | collective-permute-done | bytes 147488 | tf_op jit(solution)/shard_map/ppermute | solution.py:692
  124.0 1.8 %collective-permute-done.30 = bf16[288,256]{1,0:T(8,128)(2,1)S(1)} collective-permute-done((bf16[288,256]{1,0:T(8,128)(2,1)S(1)}, bf16[288,256]{1,0:T(8,128)(2,1)S(1)}, u32[]{:S(2)}, u32[]{:S(2)}) %collective-permute-start.30) | collective-permute-done | bytes 147488 | tf_op jit(solution)/shard_map/ppermute | solution.py:692
  125.9 1.8 %collective-permute-start.34 = (bf16[96,512]{1,0:T(8,128)(2,1)S(1)}, bf16[96,512]{1,0:T(8,128)(2,1)S(1)}, u32[]{:S(2)}, u32[]{:S(2)}) collective-permute-start(bf16[96,512]{1,0:T(8,128)(2,1)S(1)} %fusion), channel_id=1, source_target_pairs={{0,24},{4,100},{8,0},{12,108},{16,8},{20,116},{24,16},{28,124},{32... | collective-permute-start | bytes 294920 | tf_op jit(solution)/shard_map/ppermute | solution.py:618
  128.4 1.9 %collective-permute-done.34 = bf16[96,512]{1,0:T(8,128)(2,1)S(1)} collective-permute-done((bf16[96,512]{1,0:T(8,128)(2,1)S(1)}, bf16[96,512]{1,0:T(8,128)(2,1)S(1)}, u32[]{:S(2)}, u32[]{:S(2)}) %collective-permute-start.34) | collective-permute-done | bytes 98336 | tf_op jit(solution)/shard_map/ppermute | solution.py:618
  130.3 2.5 %collective-permute-done.33 = bf16[96,512]{1,0:T(8,128)(2,1)S(1)} collective-permute-done((bf16[96,512]{1,0:T(8,128)(2,1)S(1)}, bf16[96,512]{1,0:T(8,128)(2,1)S(1)}, u32[]{:S(2)}, u32[]{:S(2)}) %collective-permute-start.33) | collective-permute-done | bytes 98336 | tf_op jit(solution)/shard_map/ppermute | solution.py:618
  133.6 4.4 %collective-permute-start.35 = (bf16[384,512]{1,0:T(8,128)(2,1)S(1)}, bf16[384,512]{1,0:T(8,128)(2,1)S(1)}, u32[]{:S(2)}, u32[]{:S(2)}) collective-permute-start(bf16[384,512]{1,0:T(8,128)(2,1)S(1)} %pad_maximum_fusion.4.half_ref), channel_id=1, source_target_pairs={{0,4},{4,0},{8,12},{12,8},{16,20},{20,16},{24,28},{28,24},{32,36},... | collective-permute-start | bytes 1179656 | tf_op jit(solution)/shard_map/ppermute | solution.py:590
  (105 shorter events, 36.2 us)
Async XLA Ops:
  13.5 6.1 %collective-permute-start.1 = (bf16[96,512]{1,0:T(8,128)(2,1)}, bf16[96,512]{1,0:T(8,128)(2,1)S(1)}, u32[]{:S(2)}, u32[]{:S(2)}) collective-permute-start(bf16[96,512]{1,0:T(8,128)(2,1)} %get-tuple-element.146), channel_id=1, source_target_pairs={{0,8},{4,36},{8,16},{12,44},{16,24},{20,52},{24,0},{28,60},{32,40}... | collective-permute-start | bytes 294920 | tf_op jit(solution)/shard_map/ppermute | solution.py:609
  15.2 4.3 %collective-permute-start.3 = (bf16[96,512]{1,0:T(8,128)(2,1)S(1)}, bf16[96,512]{1,0:T(8,128)(2,1)S(1)}, u32[]{:S(2)}, u32[]{:S(2)}) collective-permute-start(bf16[96,512]{1,0:T(8,128)(2,1)S(1)} %get-tuple-element.147), channel_id=1, source_target_pairs={{0,24},{4,100},{8,0},{12,108},{16,8},{20,116},{24,16},{28,124},{32... | collective-permute-start | bytes 294920 | tf_op jit(solution)/shard_map/ppermute | solution.py:609
  17.4 5.3 %collective-permute-start.2 = (bf16[96,512]{1,0:T(8,128)(2,1)S(1)}, bf16[96,512]{1,0:T(8,128)(2,1)S(1)}, u32[]{:S(2)}, u32[]{:S(2)}) collective-permute-start(bf16[96,512]{1,0:T(8,128)(2,1)S(1)} %get-tuple-element.148), channel_id=1, source_target_pairs={{0,16},{4,68},{8,24},{12,76},{16,0},{20,84},{24,8},{28,92},{32,48}... | collective-permute-start | bytes 294920 | tf_op jit(solution)/shard_map/ppermute | solution.py:609
  23.6 4.0 %collective-permute-start.6 = (bf16[96,512]{1,0:T(8,128)(2,1)S(1)}, bf16[96,512]{1,0:T(8,128)(2,1)S(1)}, u32[]{:S(2)}, u32[]{:S(2)}) collective-permute-start(bf16[96,512]{1,0:T(8,128)(2,1)S(1)} %fusion.5), channel_id=1, source_target_pairs={{0,96},{4,28},{8,104},{12,4},{16,112},{20,12},{24,120},{28,20},{32... | collective-permute-start | bytes 294920 | tf_op jit(solution)/shard_map/ppermute | solution.py:618
  25.8 5.7 %collective-permute-start.5 = (bf16[96,512]{1,0:T(8,128)(2,1)S(1)}, bf16[96,512]{1,0:T(8,128)(2,1)S(1)}, u32[]{:S(2)}, u32[]{:S(2)}) collective-permute-start(bf16[96,512]{1,0:T(8,128)(2,1)S(1)} %fusion.5), channel_id=1, source_target_pairs={{0,32},{4,12},{8,40},{12,20},{16,48},{20,28},{24,56},{28,4},{32,64... | collective-permute-start | bytes 294920 | tf_op jit(solution)/shard_map/ppermute | solution.py:618
  25.9 5.7 %collective-permute-start.4 = (bf16[96,512]{1,0:T(8,128)(2,1)S(1)}, bf16[96,512]{1,0:T(8,128)(2,1)S(1)}, u32[]{:S(2)}, u32[]{:S(2)}) collective-permute-start(bf16[96,512]{1,0:T(8,128)(2,1)S(1)} %fusion.5), channel_id=1, source_target_pairs={{0,64},{4,20},{8,72},{12,28},{16,80},{20,4},{24,88},{28,12},{32,96... | collective-permute-start | bytes 294920 | tf_op jit(solution)/shard_map/ppermute | solution.py:618
  31.6 3.8 %collective-permute-start.9 = (bf16[96,512]{1,0:T(8,128)(2,1)S(1)}, bf16[96,512]{1,0:T(8,128)(2,1)S(1)}, u32[]{:S(2)}, u32[]{:S(2)}) collective-permute-start(bf16[96,512]{1,0:T(8,128)(2,1)S(1)} %add_add_fusion.2), channel_id=1, source_target_pairs={{0,24},{4,100},{8,0},{12,108},{16,8},{20,116},{24,16},{28,124},{32... | collective-permute-start | bytes 294920 | tf_op jit(solution)/shard_map/ppermute | solution.py:618
  33.5 5.1 %collective-permute-start.8 = (bf16[96,512]{1,0:T(8,128)(2,1)S(1)}, bf16[96,512]{1,0:T(8,128)(2,1)S(1)}, u32[]{:S(2)}, u32[]{:S(2)}) collective-permute-start(bf16[96,512]{1,0:T(8,128)(2,1)S(1)} %add_add_fusion.2), channel_id=1, source_target_pairs={{0,16},{4,68},{8,24},{12,76},{16,0},{20,84},{24,8},{28,92},{32,48}... | collective-permute-start | bytes 294920 | tf_op jit(solution)/shard_map/ppermute | solution.py:618
  33.9 5.6 %collective-permute-start.7 = (bf16[96,512]{1,0:T(8,128)(2,1)S(1)}, bf16[96,512]{1,0:T(8,128)(2,1)S(1)}, u32[]{:S(2)}, u32[]{:S(2)}) collective-permute-start(bf16[96,512]{1,0:T(8,128)(2,1)S(1)} %add_add_fusion.2), channel_id=1, source_target_pairs={{0,8},{4,36},{8,16},{12,44},{16,24},{20,52},{24,0},{28,60},{32,40}... | collective-permute-start | bytes 294920 | tf_op jit(solution)/shard_map/ppermute | solution.py:618
  39.6 5.7 %collective-permute-start.10 = (bf16[128,512]{1,0:T(8,128)(2,1)S(1)}, bf16[128,512]{1,0:T(8,128)(2,1)S(1)}, u32[]{:S(2)}, u32[]{:S(2)}) collective-permute-start(bf16[128,512]{1,0:T(8,128)(2,1)S(1)} %fusion.7), channel_id=1, source_target_pairs={{0,4},{4,0},{8,12},{12,8},{16,20},{20,16},{24,28},{28,24},{32,36},... | collective-permute-start | bytes 393224 | tf_op jit(solution)/shard_map/ppermute | solution.py:590
  57.0 5.6 %collective-permute-start.13 = (bf16[96,512]{1,0:T(8,128)(2,1)S(1)}, bf16[96,512]{1,0:T(8,128)(2,1)S(1)}, u32[]{:S(2)}, u32[]{:S(2)}) collective-permute-start(bf16[96,512]{1,0:T(8,128)(2,1)S(1)} %get-tuple-element.143), channel_id=1, source_target_pairs={{0,8},{4,36},{8,16},{12,44},{16,24},{20,52},{24,0},{28,60},{32,40}... | collective-permute-start | bytes 294920 | tf_op jit(solution)/shard_map/ppermute | solution.py:609
  57.1 5.5 %collective-permute-start.15 = (bf16[96,512]{1,0:T(8,128)(2,1)S(1)}, bf16[96,512]{1,0:T(8,128)(2,1)S(1)}, u32[]{:S(2)}, u32[]{:S(2)}) collective-permute-start(bf16[96,512]{1,0:T(8,128)(2,1)S(1)} %get-tuple-element.144), channel_id=1, source_target_pairs={{0,24},{4,100},{8,0},{12,108},{16,8},{20,116},{24,16},{28,124},{32... | collective-permute-start | bytes 294920 | tf_op jit(solution)/shard_map/ppermute | solution.py:609
  59.7 5.0 %collective-permute-start.14 = (bf16[96,512]{1,0:T(8,128)(2,1)S(1)}, bf16[96,512]{1,0:T(8,128)(2,1)S(1)}, u32[]{:S(2)}, u32[]{:S(2)}) collective-permute-start(bf16[96,512]{1,0:T(8,128)(2,1)S(1)} %get-tuple-element.145), channel_id=1, source_target_pairs={{0,16},{4,68},{8,24},{12,76},{16,0},{20,84},{24,8},{28,92},{32,48}... | collective-permute-start | bytes 294920 | tf_op jit(solution)/shard_map/ppermute | solution.py:609
  64.8 4.2 %collective-permute-start.18 = (bf16[96,512]{1,0:T(8,128)(2,1)S(1)}, bf16[96,512]{1,0:T(8,128)(2,1)S(1)}, u32[]{:S(2)}, u32[]{:S(2)}) collective-permute-start(bf16[96,512]{1,0:T(8,128)(2,1)S(1)} %fusion.2), channel_id=1, source_target_pairs={{0,96},{4,28},{8,104},{12,4},{16,112},{20,12},{24,120},{28,20},{32... | collective-permute-start | bytes 294920 | tf_op jit(solution)/shard_map/ppermute | solution.py:618
  65.4 5.1 %collective-permute-start.17 = (bf16[96,512]{1,0:T(8,128)(2,1)S(1)}, bf16[96,512]{1,0:T(8,128)(2,1)S(1)}, u32[]{:S(2)}, u32[]{:S(2)}) collective-permute-start(bf16[96,512]{1,0:T(8,128)(2,1)S(1)} %fusion.2), channel_id=1, source_target_pairs={{0,64},{4,20},{8,72},{12,28},{16,80},{20,4},{24,88},{28,12},{32,96... | collective-permute-start | bytes 294920 | tf_op jit(solution)/shard_map/ppermute | solution.py:618
  66.0 5.5 %collective-permute-start.16 = (bf16[96,512]{1,0:T(8,128)(2,1)S(1)}, bf16[96,512]{1,0:T(8,128)(2,1)S(1)}, u32[]{:S(2)}, u32[]{:S(2)}) collective-permute-start(bf16[96,512]{1,0:T(8,128)(2,1)S(1)} %fusion.2), channel_id=1, source_target_pairs={{0,32},{4,12},{8,40},{12,20},{16,48},{20,28},{24,56},{28,4},{32,64... | collective-permute-start | bytes 294920 | tf_op jit(solution)/shard_map/ppermute | solution.py:618
  71.5 3.8 %collective-permute-start.21 = (bf16[96,512]{1,0:T(8,128)(2,1)S(1)}, bf16[96,512]{1,0:T(8,128)(2,1)S(1)}, u32[]{:S(2)}, u32[]{:S(2)}) collective-permute-start(bf16[96,512]{1,0:T(8,128)(2,1)S(1)} %fusion.14), channel_id=1, source_target_pairs={{0,24},{4,100},{8,0},{12,108},{16,8},{20,116},{24,16},{28,124},{32... | collective-permute-start | bytes 294920 | tf_op jit(solution)/shard_map/ppermute | solution.py:618
  72.6 5.0 %collective-permute-start.20 = (bf16[96,512]{1,0:T(8,128)(2,1)S(1)}, bf16[96,512]{1,0:T(8,128)(2,1)S(1)}, u32[]{:S(2)}, u32[]{:S(2)}) collective-permute-start(bf16[96,512]{1,0:T(8,128)(2,1)S(1)} %fusion.14), channel_id=1, source_target_pairs={{0,16},{4,68},{8,24},{12,76},{16,0},{20,84},{24,8},{28,92},{32,48}... | collective-permute-start | bytes 294920 | tf_op jit(solution)/shard_map/ppermute | solution.py:618
  73.3 5.3 %collective-permute-start.19 = (bf16[96,512]{1,0:T(8,128)(2,1)S(1)}, bf16[96,512]{1,0:T(8,128)(2,1)S(1)}, u32[]{:S(2)}, u32[]{:S(2)}) collective-permute-start(bf16[96,512]{1,0:T(8,128)(2,1)S(1)} %fusion.14), channel_id=1, source_target_pairs={{0,8},{4,36},{8,16},{12,44},{16,24},{20,52},{24,0},{28,60},{32,40}... | collective-permute-start | bytes 294920 | tf_op jit(solution)/shard_map/ppermute | solution.py:618
  78.7 7.0 %collective-permute-start.22 = (bf16[128,512]{1,0:T(8,128)(2,1)S(1)}, bf16[128,512]{1,0:T(8,128)(2,1)S(1)}, u32[]{:S(2)}, u32[]{:S(2)}) collective-permute-start(bf16[128,512]{1,0:T(8,128)(2,1)S(1)} %fusion.6), channel_id=1, source_target_pairs={{0,4},{4,0},{8,12},{12,8},{16,20},{20,16},{24,28},{28,24},{32,36},... | collective-permute-start | bytes 393224 | tf_op jit(solution)/shard_map/ppermute | solution.py:590
  103.2 3.7 %collective-permute-start.24 = (bf16[4,384,256]{2,1,0:T(8,128)(2,1)S(1)}, bf16[4,384,256]{2,1,0:T(8,128)(2,1)S(1)}, u32[]{:S(2)}, u32[]{:S(2)}) collective-permute-start(bf16[4,384,256]{2,1,0:T(8,128)(2,1)S(1)} %get-tuple-element.126), channel_id=1, source_target_pairs={{0,4},{4,0},{8,12},{12,8},{16,20},{20,16},{24,28},{28,24},{32,36},... | collective-permute-start | bytes 2359304 | tf_op jit(solution)/shard_map/ppermute | solution.py:590
  103.6 3.3 %collective-permute-start.25 = (bf16[4,192,256]{2,1,0:T(8,128)(2,1)S(1)}, bf16[4,192,256]{2,1,0:T(8,128)(2,1)S(1)}, u32[]{:S(2)}, u32[]{:S(2)}) collective-permute-start(bf16[4,192,256]{2,1,0:T(8,128)(2,1)S(1)} %pad_maximum_fusion.3), channel_id=1, source_target_pairs={{0,4},{4,0},{8,12},{12,8},{16,20},{20,16},{24,28},{28,24},{32,36},... | collective-permute-start | bytes 1179656 | tf_op jit(solution)/shard_map/ppermute | solution.py:590
  107.1 10.3 %collective-permute-start.26 = (bf16[576,256]{1,0:T(8,128)(2,1)S(1)}, bf16[576,256]{1,0:T(8,128)(2,1)S(1)}, u32[]{:S(2)}, u32[]{:S(2)}) collective-permute-start(bf16[576,256]{1,0:T(8,128)(2,1)S(1)} %get-tuple-element.132), channel_id=1, source_target_pairs={{0,8},{4,36},{8,16},{12,44},{16,24},{20,52},{24,0},{28,60},{32,40}... | collective-permute-start | bytes 884744 | tf_op jit(solution)/shard_map/ppermute | solution.py:690
  107.2 10.2 %collective-permute-start.27 = (bf16[576,256]{1,0:T(8,128)(2,1)S(1)}, bf16[576,256]{1,0:T(8,128)(2,1)S(1)}, u32[]{:S(2)}, u32[]{:S(2)}) collective-permute-start(bf16[576,256]{1,0:T(8,128)(2,1)S(1)} %get-tuple-element.133), channel_id=1, source_target_pairs={{0,16},{4,68},{8,24},{12,76},{16,0},{20,84},{24,8},{28,92},{32,48}... | collective-permute-start | bytes 884744 | tf_op jit(solution)/shard_map/ppermute | solution.py:690
  109.0 9.1 %collective-permute-start.28 = (bf16[576,256]{1,0:T(8,128)(2,1)S(1)}, bf16[576,256]{1,0:T(8,128)(2,1)S(1)}, u32[]{:S(2)}, u32[]{:S(2)}) collective-permute-start(bf16[576,256]{1,0:T(8,128)(2,1)S(1)} %get-tuple-element.134), channel_id=1, source_target_pairs={{0,24},{4,100},{8,0},{12,108},{16,8},{20,116},{24,16},{28,124},{32... | collective-permute-start | bytes 884744 | tf_op jit(solution)/shard_map/ppermute | solution.py:690
  118.3 5.7 %collective-permute-start.29 = (bf16[288,256]{1,0:T(8,128)(2,1)S(1)}, bf16[288,256]{1,0:T(8,128)(2,1)S(1)}, u32[]{:S(2)}, u32[]{:S(2)}) collective-permute-start(bf16[288,256]{1,0:T(8,128)(2,1)S(1)} %get-tuple-element.136), channel_id=1, source_target_pairs={{0,64},{4,20},{8,72},{12,28},{16,80},{20,4},{24,88},{28,12},{32,96... | collective-permute-start | bytes 442376 | tf_op jit(solution)/shard_map/ppermute | solution.py:692
  119.1 6.7 %collective-permute-start.30 = (bf16[288,256]{1,0:T(8,128)(2,1)S(1)}, bf16[288,256]{1,0:T(8,128)(2,1)S(1)}, u32[]{:S(2)}, u32[]{:S(2)}) collective-permute-start(bf16[288,256]{1,0:T(8,128)(2,1)S(1)} %get-tuple-element.137), channel_id=1, source_target_pairs={{0,32},{4,12},{8,40},{12,20},{16,48},{20,28},{24,56},{28,4},{32,64... | collective-permute-start | bytes 442376 | tf_op jit(solution)/shard_map/ppermute | solution.py:692
  120.1 5.7 %collective-permute-start.31 = (bf16[288,256]{1,0:T(8,128)(2,1)S(1)}, bf16[288,256]{1,0:T(8,128)(2,1)S(1)}, u32[]{:S(2)}, u32[]{:S(2)}) collective-permute-start(bf16[288,256]{1,0:T(8,128)(2,1)S(1)} %get-tuple-element.138), channel_id=1, source_target_pairs={{0,96},{4,28},{8,104},{12,4},{16,112},{20,12},{24,120},{28,20},{32... | collective-permute-start | bytes 442376 | tf_op jit(solution)/shard_map/ppermute | solution.py:692
  125.9 4.4 %collective-permute-start.34 = (bf16[96,512]{1,0:T(8,128)(2,1)S(1)}, bf16[96,512]{1,0:T(8,128)(2,1)S(1)}, u32[]{:S(2)}, u32[]{:S(2)}) collective-permute-start(bf16[96,512]{1,0:T(8,128)(2,1)S(1)} %fusion), channel_id=1, source_target_pairs={{0,24},{4,100},{8,0},{12,108},{16,8},{20,116},{24,16},{28,124},{32... | collective-permute-start | bytes 294920 | tf_op jit(solution)/shard_map/ppermute | solution.py:618
  127.7 5.1 %collective-permute-start.33 = (bf16[96,512]{1,0:T(8,128)(2,1)S(1)}, bf16[96,512]{1,0:T(8,128)(2,1)S(1)}, u32[]{:S(2)}, u32[]{:S(2)}) collective-permute-start(bf16[96,512]{1,0:T(8,128)(2,1)S(1)} %fusion), channel_id=1, source_target_pairs={{0,16},{4,68},{8,24},{12,76},{16,0},{20,84},{24,8},{28,92},{32,48}... | collective-permute-start | bytes 294920 | tf_op jit(solution)/shard_map/ppermute | solution.py:618
  127.7 5.7 %collective-permute-start.32 = (bf16[96,512]{1,0:T(8,128)(2,1)S(1)}, bf16[96,512]{1,0:T(8,128)(2,1)S(1)}, u32[]{:S(2)}, u32[]{:S(2)}) collective-permute-start(bf16[96,512]{1,0:T(8,128)(2,1)S(1)} %fusion), channel_id=1, source_target_pairs={{0,8},{4,36},{8,16},{12,44},{16,24},{20,52},{24,0},{28,60},{32,40}... | collective-permute-start | bytes 294920 | tf_op jit(solution)/shard_map/ppermute | solution.py:618
  133.6 5.8 %collective-permute-start.35 = (bf16[384,512]{1,0:T(8,128)(2,1)S(1)}, bf16[384,512]{1,0:T(8,128)(2,1)S(1)}, u32[]{:S(2)}, u32[]{:S(2)}) collective-permute-start(bf16[384,512]{1,0:T(8,128)(2,1)S(1)} %pad_maximum_fusion.4.half_ref), channel_id=1, source_target_pairs={{0,4},{4,0},{8,12},{12,8},{16,20},{20,16},{24,28},{28,24},{32,36},... | collective-permute-start | bytes 1179656 | tf_op jit(solution)/shard_map/ppermute | solution.py:590
  (19 other events, 165.5 us)
